TPU v7x, 256 devices: a whole 4x4x8 slice. The times are simulated.
256 devices in a mesh: gx: 8 (over y, core), gy: 32 (over x, z).
Axes of the slice: x: 4, y: 4, z: 8, core: 2. Of those that a mesh axis runs over, the one named last changes fastest.
Arguments:
- free_velocity: float32 [8, 32, 6, 2048], P('gx', 'gy'), may hold values from -6 to 6
- body_radius: float32 [8, 32, 2048], P('gx', 'gy'), may hold values from 0.8 to 1.25
- face_lists: int32 [8, 32, 4, 256], P('gx', 'gy'), may hold values from 0 to 2047
- corner_lists: int32 [8, 32, 4, 32], P('gx', 'gy'), may hold values from 0 to 2047
- owner_body: int32 [8, 32, 4096], P('gx', 'gy'), may hold values from 0 to 2047
- other_body: int32 [8, 32, 4096], P('gx', 'gy'), may hold values from 0 to 3199
- contact_angles: float32 [8, 32, 2, 4096], P('gx', 'gy'), may hold values from -3.140625 to 3.140625
- contact_arms: float32 [8, 32, 2, 4096], P('gx', 'gy'), may hold values from 0.8 to 1.25
- friction: float32 [8, 32, 4096], P('gx', 'gy'), may hold values from 0.2 to 0.6
- approach: float32 [8, 32, 4096], P('gx', 'gy'), may hold values from -3 to 3
- start_impulse: float32 [8, 32, 3, 4096], P('gx', 'gy'), may hold values from -3 to 3
Outputs:
- velocity: float32 [8, 32, 6, 2048], P('gx', 'gy')
- impulse: float32 [8, 32, 3, 4096], P('gx', 'gy')
Inputs may be any that keep to these rules, and one draw needn't show every extreme that they name: `other_body`: columns below 2048 of the extended table are owned spheres; the rest are the copy blocks in the order of the statement. `face_lists`: indices of owned spheres; a sphere may stand in several lists. `corner_lists`: indices of owned spheres. `owner_body`: indices of owned spheres.
All inputs are finite; a program needn't handle non-finite values.
Results may differ from a plain program's by a relative error of at most 0.0003.
Values sent between devices are 32-bit elements; how exact they have to be, the bound alone decides.
No kernel may reach another device: no remote copies, remote signals or barrier semaphores. Data moves between devices by JAX's collectives and lax.ppermute only.
A program may use at most 64 MiB of HBM per device.

v0:
```python
import jax
import jax.numpy as jnp
from jax import lax
from jax.experimental import pallas as pl
from jax.experimental.pallas import tpu as pltpu
from jax.sharding import PartitionSpec as P

SWEEPS = 4
RELAX = 0.25
SMALLEST = 1e-20

BODY = 2048
FACE = 256
CORNER = 32
CONTACTS = 4096
ROWS = CONTACTS // 128
LISTED = 4 * FACE + 4 * CORNER
LIST_ROWS = LISTED // 128
OWN_TILES = BODY // 128
WIDE = 256
OWN_WIDE = BODY // WIDE
GHOST_WIDE = 6
IMPULSE_ROWS = 3 * ROWS
MESSAGE = FACE + 128

F32 = jnp.float32
BF16 = jnp.bfloat16
I32 = jnp.int32

PLANES = (
    "n0", "n1", "n2", "a0", "a1", "b0", "b1", "b2",
    "arm0", "arm1", "relax", "mu", "bias",
)
PLANE = {name: place for place, name in enumerate(PLANES)}


def lanes_of(table, lane):
    numbers = lax.GatherDimensionNumbers(
        offset_dims=(),
        collapsed_slice_dims=(1,),
        start_index_map=(1,),
        operand_batching_dims=(0,),
        start_indices_batching_dims=(0,),
    )
    return lax.gather(
        table, lane[..., None], numbers, (1, 1),
        mode=lax.GatherScatterMode.PROMISE_IN_BOUNDS,
    )


def iota(shape, dim):
    return lax.broadcasted_iota(I32, shape, dim)


def halves(values):
    high = values.astype(BF16).astype(F32)
    return high, values - high


def plane(ref, number):
    return ref[number * ROWS:(number + 1) * ROWS, :]


def spread(ref, high_row, parts, blocks, column):
    picks = [high_row == block for block in blocks]
    for part, value in enumerate(parts):
        zero = jnp.zeros_like(value)
        for pair in range(len(blocks) // 2):
            both = jnp.concatenate(
                [
                    jnp.where(picks[2 * pair], value, zero),
                    jnp.where(picks[2 * pair + 1], value, zero),
                ],
                axis=0,
            )
            start = part * len(blocks) * 8 + pair * 16
            ref[start:start + 16, column:column + 128] = both.astype(BF16)


OWN_BLOCKS = tuple(range(OWN_WIDE))
GHOST_BLOCKS = tuple(range(OWN_WIDE, OWN_WIDE + GHOST_WIDE))


def lane_hot(ref, low, rows):
    turned = jnp.transpose(low)
    along = iota((128, WIDE), 1)
    for row in range(rows):
        hot = jnp.broadcast_to(turned[:, row:row + 1], (128, WIDE)) == along
        ref[row * 128:(row + 1) * 128, :] = jnp.where(hot, 1.0, 0.0).astype(BF16)


def product(left, hot, blocks):
    total = jnp.dot(left[...], hot, preferred_element_type=F32)
    return total[:blocks * 8] + total[blocks * 8:]


def end_pulses(impulse, table, near_out, far_out):
    p0, p1, p2 = impulse
    get = lambda name: plane(table, PLANE[name])
    a0, a1 = get("a0"), get("a1")
    b0, b1, b2 = get("b0"), get("b1"), get("b2")
    force = (
        p0 * get("n0") + p1 * a0 + p2 * b0,
        p0 * get("n1") + p1 * a1 + p2 * b1,
        p0 * get("n2") + p2 * b2,
    )
    twist = (p1 * b0 - p2 * a0, p1 * b1 - p2 * a1, p1 * b2)
    arm0, arm1 = -get("arm0"), -get("arm1")
    for comp in range(3):
        near_out[pl.ds(comp, ROWS, stride=8), :] = force[comp]
        far_out[pl.ds(comp, ROWS, stride=8), :] = -force[comp]
        near_out[pl.ds(comp + 3, ROWS, stride=8), :] = arm0 * twist[comp]
        far_out[pl.ds(comp + 3, ROWS, stride=8), :] = arm1 * twist[comp]
    for comp in (6, 7):
        near_out[pl.ds(comp, ROWS, stride=8), :] = jnp.zeros((ROWS, 128), F32)
        far_out[pl.ds(comp, ROWS, stride=8), :] = jnp.zeros((ROWS, 128), F32)


def spread_rows(left, values, high, blocks):
    for row in range(ROWS):
        value = values[row * 8:(row + 1) * 8, :]
        spread(left, high[row:row + 1, :], halves(value), blocks, row * 128)


def ghost_pulses(flags, far, high_far, hot_far, gx_sends, gy_faces, left_ghost):
    spread_rows(left_ghost, far, high_far, GHOST_BLOCKS)
    total = product(left_ghost, hot_far[...], GHOST_WIDE)
    ghost = [total[block * 8:block * 8 + 8] for block in range(5)]
    send_gx(flags, ghost[0], ghost[1], ghost[4][:, :128], gx_sends)
    send_gy(flags, ghost[2], ghost[3], gy_faces)


def flag(flags, number, width=128):
    return jnp.broadcast_to(flags[number:number + 1, :1] > 0, (8, width))


def send_gx(flags, face0, face1, corners, sends):
    first, second = sends
    slot = iota((8, 128), 1) // CORNER
    to_down = (slot == 0) | (slot == 2)
    up = jnp.where(to_down | ~flag(flags, 0), 0.0, corners)
    down = jnp.where(to_down & flag(flags, 1), corners, 0.0)
    first[:, :FACE] = face1
    first[:, FACE:] = down
    second[:, :FACE] = face0
    second[:, FACE:] = up


def send_gy(flags, face2, face3, faces):
    wide = flag(flags, 6, FACE)
    faces[0][...] = jnp.where(wide, face3, face2)
    faces[1][...] = jnp.where(wide, face2, face3)


def prepare(
    flags, angles_in, arms_in, mu_in, bias_in, impulse_in, owner_in, other_in,
    radius_in, faces_in, corners_in, base_in,
    table, places, high_far, impulse, hot_far, near_values, far_values,
    gx_first, gx_second, gy_first, gy_second,
    owner, radius, faces, corners, base,
    angles, arms, mu, bias, other, flat, left_ghost, sems,
):
    copies = [
        pltpu.make_async_copy(source, target, sems.at[number])
        for number, (source, target) in enumerate((
            (other_in, other), (angles_in, angles), (arms_in, arms), (mu_in, mu),
            (bias_in, bias), (impulse_in, impulse), (owner_in, owner), (radius_in, radius),
            (faces_in, faces), (corners_in, corners), (base_in, base),
        ))
    ]
    for copy in copies:
        copy.start()
    copies[0].wait()
    far_id = other[...]
    extra = far_id - (BODY + 4 * FACE)
    block = extra >> 5
    slot = ((block & 1) << 1) | (block >> 1)
    in_block = extra & (CORNER - 1)
    is_corner = extra >= 0
    places[2 * ROWS:3 * ROWS, :] = far_id >> 7
    places[3 * ROWS:, :] = jnp.where(is_corner, slot * CORNER + in_block, far_id & 127)
    high_far[...] = far_id >> 8
    lane_hot(
        hot_far, jnp.where(is_corner, (3 - slot) * CORNER + in_block, far_id & 255), ROWS
    )
    for copy in copies[1:]:
        copy.wait()
    near_id = owner[...]
    places[:ROWS, :] = near_id >> 7
    places[ROWS:2 * ROWS, :] = near_id & 127
    for row in range(ROWS):
        cut = slice(row * 128, (row + 1) * 128)
        flat[pl.ds(row, 2, stride=ROWS), :] = angles[:, cut]
        flat[pl.ds(2 * ROWS + row, 2, stride=ROWS), :] = arms[:, cut]
    polar, azim = plane(flat, 0), plane(flat, 1)
    arm0, arm1 = plane(flat, 2), plane(flat, 3)
    cos_polar, sin_polar = jnp.cos(polar), jnp.sin(polar)
    cos_azim, sin_azim = jnp.cos(azim), jnp.sin(azim)
    cubed0 = arm0 * arm0 * arm0
    cubed1 = arm1 * arm1 * arm1
    values = {
        "n0": cos_polar * cos_azim, "n1": cos_polar * sin_azim, "n2": sin_polar,
        "a0": -sin_azim, "a1": cos_azim,
        "b0": -sin_polar * cos_azim, "b1": -sin_polar * sin_azim, "b2": cos_polar,
        "arm0": arm0, "arm1": arm1,
        "relax": RELAX / (1.0 / cubed0 + 1.0 / cubed1),
        "mu": mu[...], "bias": bias[...],
    }
    for name, value in values.items():
        number = PLANE[name]
        table[number * ROWS:(number + 1) * ROWS, :] = value
    end_pulses([plane(impulse, comp) for comp in range(3)], table, near_values, far_values)
    ghost_pulses(
        flags, far_values, high_far, hot_far, (gx_first, gx_second), (gy_first, gy_second), left_ghost
    )


def prepare_own(
    near_values, owner, radius, faces, corners, base_rows,
    pulse, high_near, hot_near, hot_list, list_places, inverse, base,
    left_near,
):
    near_id = owner[...]
    high_near[...] = near_id >> 8
    lane_hot(hot_near, near_id & 255, ROWS)
    for number in range(4):
        for part in range(2):
            row = number * 2 + part
            list_places[row:row + 1, :] = faces[number:number + 1, part * 128:(part + 1) * 128]
    for place, number in enumerate((0, 2, 1, 3)):
        list_places[8:9, place * CORNER:(place + 1) * CORNER] = corners[number:number + 1, :]
    for place, number in enumerate((3, 1, 2, 0)):
        list_places[9:10, place * CORNER:(place + 1) * CORNER] = corners[number:number + 1, :]
    list_places[10:, :] = jnp.zeros((6, 128), I32)
    lane_hot(hot_list, list_places[...] & 255, LIST_ROWS)

    size = radius[...]
    cubed = size * size * size
    linear = 1.0 / cubed
    angular = 2.5 / (cubed * size * size)
    inverse[...] = jnp.where(iota((8, BODY), 0) < 3, linear, angular)
    for tile in range(OWN_TILES):
        base[:, tile * 128:(tile + 1) * 128] = base_rows[pl.ds(tile, 6, stride=OWN_TILES), :]
    scatter_near(near_values, high_near, hot_near, pulse, left_near)


def store_blocks(pulse, total):
    for block in range(OWN_WIDE):
        pulse[:, block * WIDE:(block + 1) * WIDE] = total[block * 8:block * 8 + 8]


def scatter_near(values, high_near, hot_near, pulse, left_near):
    spread_rows(left_near, values, high_near, OWN_BLOCKS)
    store_blocks(pulse, product(left_near, hot_near[...], OWN_WIDE))


def masked(flags, number, value):
    return jnp.where(flags[number:number + 1, :] > 0, value, jnp.zeros_like(value))


def gx_tiles(flags, first, second):
    return [
        masked(flags, number, ref[:, part * 128:(part + 1) * 128])
        for number, ref in enumerate((first, second))
        for part in range(2)
    ]


def gy_tiles(flags, first, second):
    tiles = []
    for part in range(2):
        cut = slice(part * 128, (part + 1) * 128)
        one, two = first[:, cut], second[:, cut]
        tiles.append((jnp.where(flag(flags, 6), one, two), jnp.where(flag(flags, 6), two, one)))
    left, right = zip(*tiles)
    corners = jnp.where(flags[7:8, :] > 0, first[:, FACE:], second[:, FACE:])
    return (
        [masked(flags, 2, tile) for tile in left] + [masked(flags, 3, tile) for tile in right]
        + [masked(flags, 4, corners)]
    )


def list_product(left_list, tiles, list_places, hot, first):
    for row, tile in enumerate(tiles):
        high_row = list_places[first + row:first + row + 1, :] >> 8
        spread(left_list, high_row, halves(tile), OWN_BLOCKS, row * 128)
    rows = slice(first * 128, (first + len(tiles)) * 128)
    return product(left_list, hot[rows, :], OWN_WIDE)


def scatter_far(
    flags, values, high_far, hot_far, near_pulse, list_places, hot_list, from_up, from_down,
    pulse, left_far, left_list,
):
    spread_rows(left_far, values, high_far, OWN_BLOCKS)
    total = product(left_far, hot_far[...], OWN_WIDE)
    total = total + list_product(
        left_list, gx_tiles(flags, from_up, from_down), list_places, hot_list, 0
    )
    for block in range(OWN_WIDE):
        cut = slice(block * WIDE, (block + 1) * WIDE)
        pulse[:, cut] = near_pulse[:, cut] + total[block * 8:block * 8 + 8]


def settled(flags, own, inverse, base, list_places, hot_list, from_left, from_right, left_list):
    added = list_product(
        left_list, gy_tiles(flags, from_left, from_right), list_places, hot_list, 4
    )
    blocks = []
    for block in range(OWN_WIDE):
        cut = slice(block * WIDE, (block + 1) * WIDE)
        total = own[:6, cut] + added[block * 8:block * 8 + 6]
        blocks.append(base[:, cut] + inverse[:6, cut] * total)
    return blocks


def listed(velocity, list_places, row):
    entry = jnp.broadcast_to(list_places[row:row + 1, :], (8, 128))
    tile_id, lane = entry >> 7, entry & 127
    total = jnp.zeros((8, 128), F32)
    for tile in range(OWN_TILES):
        table = velocity[:, tile * 128:(tile + 1) * 128]
        total = jnp.where(tile_id == tile, lanes_of(table, lane), total)
    return total


def settle(
    flags, own, inverse, base, list_places, hot_list, from_left, from_right,
    velocity, gx_first, gx_second, left_list,
):
    blocks = settled(
        flags, own, inverse, base, list_places, hot_list, from_left, from_right, left_list
    )
    zero = jnp.zeros((2, WIDE), F32)
    for block, value in enumerate(blocks):
        velocity[:, block * WIDE:(block + 1) * WIDE] = jnp.concatenate([value, zero], axis=0)
    found = [listed(velocity, list_places, row) for row in (0, 1, 2, 3, 9)]
    face = [jnp.concatenate(found[2 * k:2 * k + 2], axis=1) for k in range(2)]
    send_gx(flags, *face, found[4], (gx_first, gx_second))


def settle_last(
    flags, own, inverse, base, list_places, hot_list, from_left, from_right,
    velocity, left_list,
):
    blocks = settled(
        flags, own, inverse, base, list_places, hot_list, from_left, from_right, left_list
    )
    for block, value in enumerate(blocks):
        for part in range(2):
            tile = 2 * block + part
            velocity[pl.ds(tile, 6, stride=OWN_TILES), :] = value[:, part * 128:(part + 1) * 128]


def pick(tables, tile_id, lane, firsts, totals):
    for tile, table in zip(firsts, tables):
        here = tile_id == tile
        for comp in range(6):
            row = jnp.broadcast_to(table[comp:comp + 1, :], (ROWS, 128))
            totals[comp] = jnp.where(here, lanes_of(row, lane), totals[comp])
    return totals


def own_tables(velocity):
    return [velocity[:, tile * 128:(tile + 1) * 128] for tile in range(OWN_TILES)]


def blank():
    return [jnp.zeros((ROWS, 128), F32) for _ in range(6)]


def gather_near(flags, velocity, places, list_places, near, gy_first, gy_second):
    tiles = [listed(velocity, list_places, row) for row in range(4, 8)]
    send_gy(
        flags, jnp.concatenate(tiles[:2], axis=1), jnp.concatenate(tiles[2:], axis=1),
        (gy_first, gy_second),
    )
    found = pick(
        own_tables(velocity), places[:ROWS, :], places[ROWS:2 * ROWS, :], range(OWN_TILES), blank()
    )
    for comp in range(6):
        near[comp * ROWS:(comp + 1) * ROWS, :] = found[comp]


def gather_far(flags, velocity, places, from_up, from_down, far):
    found = pick(
        own_tables(velocity) + gx_tiles(flags, from_up, from_down),
        places[2 * ROWS:3 * ROWS, :], places[3 * ROWS:, :], range(OWN_TILES + 4), blank(),
    )
    for comp in range(6):
        far[comp * ROWS:(comp + 1) * ROWS, :] = found[comp]


def sweep(
    flags, near_ref, far_ref, table, places, high_far, hot_far, impulse, from_left, from_right,
    impulse_out, near_values, far_values, gx_first, gx_second, gy_first, gy_second, left_ghost,
):
    near = [plane(near_ref, comp) for comp in range(6)]
    far = pick(
        gy_tiles(flags, from_left, from_right),
        places[2 * ROWS:3 * ROWS, :], places[3 * ROWS:, :],
        range(OWN_TILES + 4, OWN_TILES + 9), [plane(far_ref, comp) for comp in range(6)],
    )
    get = lambda name: plane(table, PLANE[name])
    n0, n1, n2 = get("n0"), get("n1"), get("n2")
    a0, a1 = get("a0"), get("a1")
    b0, b1, b2 = get("b0"), get("b1"), get("b2")
    arm0, arm1, relax, mu = get("arm0"), get("arm1"), get("relax"), get("mu")
    w0, w1, w2 = [near[c] - far[c] for c in range(3)]
    s0, s1, s2 = [arm0 * near[c] + arm1 * far[c] for c in range(3, 6)]
    rate_n = n0 * w0 + n1 * w1 + n2 * w2
    rate_a = (a0 * w0 + a1 * w1) - (b0 * s0 + b1 * s1 + b2 * s2)
    rate_b = (b0 * w0 + b1 * w1 + b2 * w2) + (a0 * s0 + a1 * s1)
    trial_n = plane(impulse, 0) - relax * (rate_n + get("bias"))
    trial_a = plane(impulse, 1) - relax * rate_a
    trial_b = plane(impulse, 2) - relax * rate_b
    length = jnp.sqrt(trial_a * trial_a + trial_b * trial_b)
    inside = length <= mu * trial_n
    dead = mu * length <= -trial_n
    level = (trial_n + mu * length) / (1.0 + mu * mu)
    factor = mu * level / jnp.maximum(length, SMALLEST)
    choose = lambda kept, cone: jnp.where(inside, kept, jnp.where(dead, 0.0, cone))
    fresh = [
        choose(trial_n, level), choose(trial_a, factor * trial_a), choose(trial_b, factor * trial_b)
    ]
    for comp in range(3):
        impulse_out[comp * ROWS:(comp + 1) * ROWS, :] = fresh[comp]
    end_pulses(fresh, table, near_values, far_values)
    ghost_pulses(
        flags, far_values, high_far, hot_far, (gx_first, gx_second), (gy_first, gy_second), left_ghost
    )


def shape(*dims, kind=F32):
    return jax.ShapeDtypeStruct(dims, kind)


FACES = (shape(8, FACE), shape(8, FACE))
GX_SENDS = (shape(8, MESSAGE), shape(8, MESSAGE))
VALUES = shape(8 * ROWS, 128)
PULSE = shape(8, BODY)
LEFT_OWN = pltpu.VMEM((2 * OWN_WIDE * 8, CONTACTS), BF16)
LEFT_GHOST = pltpu.VMEM((2 * GHOST_WIDE * 8, CONTACTS), BF16)


def left_list(tiles):
    return pltpu.VMEM((2 * OWN_WIDE * 8, tiles * 128), BF16)


def call(body, outs, scratch, *operands, specs=None):
    vmem = pl.BlockSpec(memory_space=pltpu.VMEM)
    return pl.pallas_call(
        body,
        out_shape=outs,
        in_specs=specs or [vmem] * len(operands),
        out_specs=[vmem] * len(outs),
        scratch_shapes=scratch,
        compiler_params=pltpu.CompilerParams(vmem_limit_bytes=10 * 1024 * 1024),
    )(*operands)


def loop(value, back, lines, place):
    count, length = lines
    pairs = []
    for line in range(0, count, 2):
        ring = [place(line, step) for step in range(length)]
        ring += [place(line + 1, step) for step in reversed(range(length))]
        for here, there in zip(ring, ring[1:] + ring[:1]):
            pairs.append((there, here) if back else (here, there))
    return lax.ppermute(value, ("gx", "gy"), pairs)


def along_gx(first, second):
    size = lax.axis_size("gx")
    down = [(i, (i + 1) % size) for i in range(size)]
    up = [(j, i) for i, j in down]
    return lax.ppermute(first, "gx", down), lax.ppermute(second, "gx", up)


def along_gy(got_first, got_second, face_first, face_second):
    rows, columns = lax.axis_size("gx"), lax.axis_size("gy")
    corners = got_first[:, FACE:] + got_second[:, FACE:]
    first = jnp.concatenate([face_first, corners], axis=1)
    second = jnp.concatenate([face_second, corners], axis=1)
    place = lambda line, step: line * columns + step
    lines = (rows, columns)
    return loop(first, False, lines, place), loop(second, True, lines, place)


def presence():
    row_at, row_count = lax.axis_index("gx"), lax.axis_size("gx")
    col_at, col_count = lax.axis_index("gy"), lax.axis_size("gy")
    row, slot = iota((8, 128), 0), iota((8, 128), 1) // CORNER
    above = (row == 0) | ((row == 4) & ((slot == 0) | (slot == 2)))
    below = (row == 1) | ((row == 4) & ((slot == 1) | (slot == 3)))
    before = (row == 2) | ((row == 4) & (slot < 2))
    after = (row == 3) | ((row == 4) & (slot >= 2))
    odd_row = lax.rem(row_at, 2)
    off = (
        (above & (row_at == 0)) | (below & (row_at == row_count - 1))
        | (before & (col_at == 0)) | (after & (col_at == col_count - 1))
        | ((row == 6) & (odd_row == 1))
        | ((row == 7) & ((slot >> 1) != odd_row))
    )
    return jnp.where(off, 0.0, 1.0)


def shards(
    free_velocity, body_radius, face_lists, corner_lists, owner_body, other_body,
    contact_angles, contact_arms, friction, approach, start_impulse,
):
    flags = presence()
    in_rows = lambda value: value[0, 0].reshape(-1, 128)
    dma = pltpu.SemaphoreType.DMA
    raw = [
        pltpu.with_memory_space_constraint(value, pltpu.HBM)
        for value in (
            contact_angles[0, 0], contact_arms[0, 0], in_rows(friction), in_rows(approach),
            in_rows(start_impulse), in_rows(owner_body), in_rows(other_body),
            body_radius[0], face_lists[0, 0], corner_lists[0, 0], in_rows(free_velocity),
        )
    ]
    (
        table, places, high_far, impulse, hot_far, near_values, far_values,
        gx_first, gx_second, gy_first, gy_second, owner, radius, faces, corners, base_rows,
    ) = call(
        prepare,
        (
            shape(len(PLANES) * ROWS, 128),
            shape(4 * ROWS, 128, kind=I32),
            shape(ROWS, 128, kind=I32),
            shape(IMPULSE_ROWS, 128),
            shape(CONTACTS, WIDE, kind=BF16),
            VALUES, VALUES,
        ) + GX_SENDS + FACES + (
            shape(ROWS, 128, kind=I32),
            shape(1, BODY),
            shape(4, FACE, kind=I32),
            shape(4, CORNER, kind=I32),
            shape(6 * OWN_TILES, 128),
        ),
        (
            pltpu.VMEM((2, CONTACTS), F32),
            pltpu.VMEM((2, CONTACTS), F32),
            pltpu.VMEM((ROWS, 128), F32),
            pltpu.VMEM((ROWS, 128), F32),
            pltpu.VMEM((ROWS, 128), I32),
            pltpu.VMEM((4 * ROWS, 128), F32),
            LEFT_GHOST,
            dma((11,)),
        ),
        flags, *raw,
        specs=[pl.BlockSpec(memory_space=pltpu.VMEM)]
        + [pl.BlockSpec(memory_space=pltpu.HBM)] * len(raw),
    )
    for number in range(SWEEPS + 1):
        got = along_gx(gx_first, gx_second)
        if number == 0:
            pulse, high_near, hot_near, hot_list, list_places, inverse, base = call(
                prepare_own,
                (
                    PULSE,
                    shape(ROWS, 128, kind=I32),
                    shape(CONTACTS, WIDE, kind=BF16),
                    shape(LISTED, WIDE, kind=BF16),
                    shape(16, 128, kind=I32),
                    PULSE,
                    shape(6, BODY),
                ),
                (LEFT_OWN,),
                near_values, owner, radius, faces, corners, base_rows,
            )
        else:
            (pulse,) = call(
                scatter_near, (PULSE,), (LEFT_OWN,), near_values, high_near, hot_near
            )
        got_gy = along_gy(*got, gy_first, gy_second)
        (own,) = call(
            scatter_far, (PULSE,), (LEFT_OWN, left_list(4)),
            flags, far_values, high_far, hot_far, pulse, list_places, hot_list, *got,
        )
        fixed = (flags, own, inverse, base, list_places, hot_list, *got_gy)
        if number == SWEEPS:
            (velocity,) = call(
                settle_last, (shape(6 * OWN_TILES, 128),), (left_list(5),), *fixed
            )
            break
        velocity, gx_first, gx_second = call(
            settle, (PULSE,) + GX_SENDS, (left_list(5),), *fixed
        )
        got = along_gx(gx_first, gx_second)
        near, gy_first, gy_second = call(
            gather_near, (shape(6 * ROWS, 128),) + FACES, (), flags, velocity, places, list_places
        )
        got_gy = along_gy(*got, gy_first, gy_second)
        (far,) = call(
            gather_far, (shape(6 * ROWS, 128),), (), flags, velocity, places, *got
        )
        impulse, near_values, far_values, gx_first, gx_second, gy_first, gy_second = call(
            sweep, (shape(IMPULSE_ROWS, 128), VALUES, VALUES) + GX_SENDS + FACES, (LEFT_GHOST,),
            flags, near, far, table, places, high_far, hot_far, impulse, *got_gy,
        )
    return velocity.reshape(1, 1, 6, BODY), impulse.reshape(1, 1, 3, CONTACTS)

def solution(mesh):
    in_specs = (
        P("gx", "gy", None, None),
        P("gx", "gy", None),
        P("gx", "gy", None, None),
        P("gx", "gy", None, None),
        P("gx", "gy", None),
        P("gx", "gy", None),
        P("gx", "gy", None, None),
        P("gx", "gy", None, None),
        P("gx", "gy", None),
        P("gx", "gy", None),
        P("gx", "gy", None, None),
    )
    out_specs = (P("gx", "gy", None, None), P("gx", "gy", None, None))
    return jax.shard_map(shards, mesh=mesh, in_specs=in_specs, out_specs=out_specs, check_vma=False)
```

profile of v0, /device:TPU:6, one launch (start us, length us, event | category | flops | bytes accessed | tf_op | source)
XLA Modules:
  0.0 118.6 jit_solution(1451752191952272813)
XLA Ops:
  0.8 2.4 %shard_map.122 = (f32[416,128]{1,0:T(8,128)S(1)}, s32[128,128]{1,0:T(8,128)S(1)}, s32[32,128]{1,0:T(8,128)S(1)}, f32[96,128]{1,0:T(8,128)S(1)}, bf16[4096,256]{1...) custom-call(f32[8,128]{1,0:T(8,128)S(1)} %fusion.3.flags, ...), custom_call_target="tpu_custom_call" | custom-call | tf_op jit(solution)/shard_map/pallas_call | solution.py:452
  3.2 2.9 %collective-permute-start.1 = (f32[8,384]{1,0:T(8,128)S(1)}, f32[8,384]{1,0:T(8,128)S(1)}, u32[]{:S(2)}, u32[]{:S(2)}) collective-permute-start(f32[8,384]{1,0:T(8,128)S(1)} %get-tuple-element.90), channel_id=1, source_target_pairs={{32,0},{64,32},{96,64},{128,96},{160,128},{192,160},{224,192},{0,2... | collective-permute-start | bytes 36872 | tf_op jit(solution)/shard_map/ppermute | solution.py:477
  6.2 1.4 %collective-permute-done.from_up = f32[8,384]{1,0:T(8,128)S(1)} collective-permute-done((f32[8,384]{1,0:T(8,128)S(1)}, f32[8,384]{1,0:T(8,128)S(1)}, u32[]{:S(2)}, u32[]{:S(2)}) %collective-permute-start) | collective-permute-done | bytes 12320 | tf_op jit(solution)/shard_map/ppermute | solution.py:477
  7.6 6.2 %collective-permute-start.3 = (f32[8,384]{1,0:T(8,128)S(1)}, f32[8,384]{1,0:T(8,128)S(1)}, u32[]{:S(2)}, u32[]{:S(2)}) collective-permute-start(f32[8,384]{1,0:T(8,128)S(1)} %get-tuple-element.172), channel_id=1, source_target_pairs={{1,0},{2,1},{3,2},{4,3},{5,4},{6,5},{7,6},{8,7},{9,8},{10,9},{11,1... | collective-permute-start | bytes 36872 | tf_op jit(solution)/shard_map/ppermute | solution.py:470
  13.8 1.4 %shard_map.123 = (f32[8,2048]{1,0:T(8,128)S(1)}, s32[32,128]{1,0:T(8,128)S(1)}, bf16[4096,256]{1,0:T(8,128)(2,1)S(1)}, bf16[1152,256]{1,0:T(8,128)(2,1)S(1)}, s3...) custom-call(f32[256,128]{1,0:T(8,128)S(1)} %get-tuple-element.80.near_values, ...), custom_call_target="tpu_custom_call" | custom-call | tf_op jit(solution)/shard_map/pallas_call | solution.py:452
  16.0 3.6 %collective-permute-done.2.from_left = f32[8,384]{1,0:T(8,128)S(1)} collective-permute-done((f32[8,384]{1,0:T(8,128)S(1)}, f32[8,384]{1,0:T(8,128)S(1)}, u32[]{:S(2)}, u32[]{:S(2)}) %collective-permute-start.2) | collective-permute-done | bytes 12320 | tf_op jit(solution)/shard_map/ppermute | solution.py:470
  20.1 2.9 %collective-permute-start.5 = (f32[8,384]{1,0:T(8,128)S(1)}, f32[8,384]{1,0:T(8,128)S(1)}, u32[]{:S(2)}, u32[]{:S(2)}) collective-permute-start(f32[8,384]{1,0:T(8,128)S(1)} %get-tuple-element.99), channel_id=1, source_target_pairs={{32,0},{64,32},{96,64},{128,96},{160,128},{192,160},{224,192},{0,2... | collective-permute-start | bytes 36872 | tf_op jit(solution)/shard_map/ppermute | solution.py:477
  23.0 1.2 %shard_map.126 = (f32[192,128]{1,0:T(8,128)S(1)}, f32[8,256]{1,0:T(8,128)S(1)}, f32[8,256]{1,0:T(8,128)S(1)}) custom-call(f32[8,128]{1,0:T(8,128)S(1)} %fusion.3.flags, f32[8,2048]{1,0:T(8,128)S(1)} %get-tuple-element.95.velocity, s32[128,128]{1,0:T(8,128)S(1)} %get-tuple-element.96.places, s32[16,128]{1,0:T(8,128)S(1)} %get-tuple-element.87.list_places), custom_call_target="tpu_custom_call" | custom-call | tf_op jit(solution)/shard_map/pallas_call | solution.py:452
  25.0 1.5 %collective-permute-start.6 = (f32[8,384]{1,0:T(8,128)S(1)}, f32[8,384]{1,0:T(8,128)S(1)}, u32[]{:S(2)}, u32[]{:S(2)}) collective-permute-start(f32[8,384]{1,0:T(8,128)S(1)} %get-tuple-element.171), channel_id=1, source_target_pairs={{0,1},{1,2},{2,3},{3,4},{4,5},{5,6},{6,7},{7,8},{8,9},{9,10},{10,1... | collective-permute-start | bytes 36872 | tf_op jit(solution)/shard_map/ppermute | solution.py:470
  26.5 1.4 %shard_map.127.far_ref = f32[192,128]{1,0:T(8,128)S(1)} custom-call(f32[8,128]{1,0:T(8,128)S(1)} %fusion.3.flags, f32[8,2048]{1,0:T(8,128)S(1)} %get-tuple-element.95.velocity, s32[128,128]{1,0:T(8,128)S(1)} %get-tuple-element.96.places, f32[8,384]{1,0:T(8,128)S(1)} %collective-permute-done.4.from_up, f32[8,384]{1,0:T(8,128)S(1)} %collective-permute-done.5.from_down), custom_call_target="tpu_custom_call" | custom-call | tf_op jit(solution)/shard_map/pallas_call | solution.py:452
  28.2 2.6 %collective-permute-done.6.from_left = f32[8,384]{1,0:T(8,128)S(1)} collective-permute-done((f32[8,384]{1,0:T(8,128)S(1)}, f32[8,384]{1,0:T(8,128)S(1)}, u32[]{:S(2)}, u32[]{:S(2)}) %collective-permute-start.6) | collective-permute-done | bytes 12320 | tf_op jit(solution)/shard_map/ppermute | solution.py:470
  30.8 0.8 shard_map.128
  31.7 2.9 %collective-permute-start.9 = (f32[8,384]{1,0:T(8,128)S(1)}, f32[8,384]{1,0:T(8,128)S(1)}, u32[]{:S(2)}, u32[]{:S(2)}) collective-permute-start(f32[8,384]{1,0:T(8,128)S(1)} %get-tuple-element.109), channel_id=1, source_target_pairs={{32,0},{64,32},{96,64},{128,96},{160,128},{192,160},{224,192},{0,2... | collective-permute-start | bytes 36872 | tf_op jit(solution)/shard_map/ppermute | solution.py:477
  34.6 1.4 %collective-permute-done.8.from_up = f32[8,384]{1,0:T(8,128)S(1)} collective-permute-done((f32[8,384]{1,0:T(8,128)S(1)}, f32[8,384]{1,0:T(8,128)S(1)}, u32[]{:S(2)}, u32[]{:S(2)}) %collective-permute-start.8) | collective-permute-done | bytes 12320 | tf_op jit(solution)/shard_map/ppermute | solution.py:477
  36.0 2.1 %collective-permute-start.11 = (f32[8,384]{1,0:T(8,128)S(1)}, f32[8,384]{1,0:T(8,128)S(1)}, u32[]{:S(2)}, u32[]{:S(2)}) collective-permute-start(f32[8,384]{1,0:T(8,128)S(1)} %get-tuple-element.168), channel_id=1, source_target_pairs={{1,0},{2,1},{3,2},{4,3},{5,4},{6,5},{7,6},{8,7},{9,8},{10,9},{11,1... | collective-permute-start | bytes 36872 | tf_op jit(solution)/shard_map/ppermute | solution.py:470
  39.8 4.2 %collective-permute-done.10.from_left = f32[8,384]{1,0:T(8,128)S(1)} collective-permute-done((f32[8,384]{1,0:T(8,128)S(1)}, f32[8,384]{1,0:T(8,128)S(1)}, u32[]{:S(2)}, u32[]{:S(2)}) %collective-permute-start.10) | collective-permute-done | bytes 12320 | tf_op jit(solution)/shard_map/ppermute | solution.py:470
  44.5 2.9 %collective-permute-start.13 = (f32[8,384]{1,0:T(8,128)S(1)}, f32[8,384]{1,0:T(8,128)S(1)}, u32[]{:S(2)}, u32[]{:S(2)}) collective-permute-start(f32[8,384]{1,0:T(8,128)S(1)} %get-tuple-element.115), channel_id=1, source_target_pairs={{32,0},{64,32},{96,64},{128,96},{160,128},{192,160},{224,192},{0,2... | collective-permute-start | bytes 36872 | tf_op jit(solution)/shard_map/ppermute | solution.py:477
  47.4 1.2 %shard_map.132 = (f32[192,128]{1,0:T(8,128)S(1)}, f32[8,256]{1,0:T(8,128)S(1)}, f32[8,256]{1,0:T(8,128)S(1)}) custom-call(f32[8,128]{1,0:T(8,128)S(1)} %fusion.3.flags, f32[8,2048]{1,0:T(8,128)S(1)} %get-tuple-element.112.velocity, s32[128,128]{1,0:T(8,128)S(1)} %get-tuple-element.96.places, s32[16,128]{1,0:T(8,128)S(1)} %get-tuple-element.87.list_places), custom_call_target="tpu_custom_call" | custom-call | tf_op jit(solution)/shard_map/pallas_call | solution.py:452
  49.4 1.5 %collective-permute-start.14 = (f32[8,384]{1,0:T(8,128)S(1)}, f32[8,384]{1,0:T(8,128)S(1)}, u32[]{:S(2)}, u32[]{:S(2)}) collective-permute-start(f32[8,384]{1,0:T(8,128)S(1)} %get-tuple-element.167), channel_id=1, source_target_pairs={{0,1},{1,2},{2,3},{3,4},{4,5},{5,6},{6,7},{7,8},{8,9},{9,10},{10,1... | collective-permute-start | bytes 36872 | tf_op jit(solution)/shard_map/ppermute | solution.py:470
  50.9 1.4 %shard_map.133.far_ref = f32[192,128]{1,0:T(8,128)S(1)} custom-call(f32[8,128]{1,0:T(8,128)S(1)} %fusion.3.flags, f32[8,2048]{1,0:T(8,128)S(1)} %get-tuple-element.112.velocity, s32[128,128]{1,0:T(8,128)S(1)} %get-tuple-element.96.places, f32[8,384]{1,0:T(8,128)S(1)} %collective-permute-done.12.from_up, f32[8,384]{1,0:T(8,128)S(1)} %collective-permute-done.13.from_down), custom_call_target="tpu_custom_call" | custom-call | tf_op jit(solution)/shard_map/pallas_call | solution.py:452
  52.6 2.7 %collective-permute-done.14.from_left = f32[8,384]{1,0:T(8,128)S(1)} collective-permute-done((f32[8,384]{1,0:T(8,128)S(1)}, f32[8,384]{1,0:T(8,128)S(1)}, u32[]{:S(2)}, u32[]{:S(2)}) %collective-permute-start.14) | collective-permute-done | bytes 12320 | tf_op jit(solution)/shard_map/ppermute | solution.py:470
  55.3 0.8 shard_map.134
  56.1 2.9 %collective-permute-start.17 = (f32[8,384]{1,0:T(8,128)S(1)}, f32[8,384]{1,0:T(8,128)S(1)}, u32[]{:S(2)}, u32[]{:S(2)}) collective-permute-start(f32[8,384]{1,0:T(8,128)S(1)} %get-tuple-element.122), channel_id=1, source_target_pairs={{32,0},{64,32},{96,64},{128,96},{160,128},{192,160},{224,192},{0,2... | collective-permute-start | bytes 36872 | tf_op jit(solution)/shard_map/ppermute | solution.py:477
  59.1 1.4 %collective-permute-done.16.from_up = f32[8,384]{1,0:T(8,128)S(1)} collective-permute-done((f32[8,384]{1,0:T(8,128)S(1)}, f32[8,384]{1,0:T(8,128)S(1)}, u32[]{:S(2)}, u32[]{:S(2)}) %collective-permute-start.16) | collective-permute-done | bytes 12320 | tf_op jit(solution)/shard_map/ppermute | solution.py:477
  60.5 2.1 %collective-permute-start.19 = (f32[8,384]{1,0:T(8,128)S(1)}, f32[8,384]{1,0:T(8,128)S(1)}, u32[]{:S(2)}, u32[]{:S(2)}) collective-permute-start(f32[8,384]{1,0:T(8,128)S(1)} %get-tuple-element.164), channel_id=1, source_target_pairs={{1,0},{2,1},{3,2},{4,3},{5,4},{6,5},{7,6},{8,7},{9,8},{10,9},{11,1... | collective-permute-start | bytes 36872 | tf_op jit(solution)/shard_map/ppermute | solution.py:470
  64.2 4.2 %collective-permute-done.18.from_left = f32[8,384]{1,0:T(8,128)S(1)} collective-permute-done((f32[8,384]{1,0:T(8,128)S(1)}, f32[8,384]{1,0:T(8,128)S(1)}, u32[]{:S(2)}, u32[]{:S(2)}) %collective-permute-start.18) | collective-permute-done | bytes 12320 | tf_op jit(solution)/shard_map/ppermute | solution.py:470
  68.9 2.9 %collective-permute-start.21 = (f32[8,384]{1,0:T(8,128)S(1)}, f32[8,384]{1,0:T(8,128)S(1)}, u32[]{:S(2)}, u32[]{:S(2)}) collective-permute-start(f32[8,384]{1,0:T(8,128)S(1)} %get-tuple-element.128), channel_id=1, source_target_pairs={{32,0},{64,32},{96,64},{128,96},{160,128},{192,160},{224,192},{0,2... | collective-permute-start | bytes 36872 | tf_op jit(solution)/shard_map/ppermute | solution.py:477
  71.9 1.2 %shard_map.138 = (f32[192,128]{1,0:T(8,128)S(1)}, f32[8,256]{1,0:T(8,128)S(1)}, f32[8,256]{1,0:T(8,128)S(1)}) custom-call(f32[8,128]{1,0:T(8,128)S(1)} %fusion.3.flags, f32[8,2048]{1,0:T(8,128)S(1)} %get-tuple-element.125.velocity, s32[128,128]{1,0:T(8,128)S(1)} %get-tuple-element.96.places, s32[16,128]{1,0:T(8,128)S(1)} %get-tuple-element.87.list_places), custom_call_target="tpu_custom_call" | custom-call | tf_op jit(solution)/shard_map/pallas_call | solution.py:452
  73.9 1.5 %collective-permute-start.22 = (f32[8,384]{1,0:T(8,128)S(1)}, f32[8,384]{1,0:T(8,128)S(1)}, u32[]{:S(2)}, u32[]{:S(2)}) collective-permute-start(f32[8,384]{1,0:T(8,128)S(1)} %get-tuple-element.163), channel_id=1, source_target_pairs={{0,1},{1,2},{2,3},{3,4},{4,5},{5,6},{6,7},{7,8},{8,9},{9,10},{10,1... | collective-permute-start | bytes 36872 | tf_op jit(solution)/shard_map/ppermute | solution.py:470
  75.4 1.4 %shard_map.139.far_ref = f32[192,128]{1,0:T(8,128)S(1)} custom-call(f32[8,128]{1,0:T(8,128)S(1)} %fusion.3.flags, f32[8,2048]{1,0:T(8,128)S(1)} %get-tuple-element.125.velocity, s32[128,128]{1,0:T(8,128)S(1)} %get-tuple-element.96.places, f32[8,384]{1,0:T(8,128)S(1)} %collective-permute-done.20.from_up, f32[8,384]{1,0:T(8,128)S(1)} %collective-permute-done.21.from_down), custom_call_target="tpu_custom_call" | custom-call | tf_op jit(solution)/shard_map/pallas_call | solution.py:452
  77.0 2.7 %collective-permute-done.22.from_left = f32[8,384]{1,0:T(8,128)S(1)} collective-permute-done((f32[8,384]{1,0:T(8,128)S(1)}, f32[8,384]{1,0:T(8,128)S(1)}, u32[]{:S(2)}, u32[]{:S(2)}) %collective-permute-start.22) | collective-permute-done | bytes 12320 | tf_op jit(solution)/shard_map/ppermute | solution.py:470
  79.7 0.8 shard_map.140
  80.5 2.9 %collective-permute-start.25 = (f32[8,384]{1,0:T(8,128)S(1)}, f32[8,384]{1,0:T(8,128)S(1)}, u32[]{:S(2)}, u32[]{:S(2)}) collective-permute-start(f32[8,384]{1,0:T(8,128)S(1)} %get-tuple-element.135), channel_id=1, source_target_pairs={{32,0},{64,32},{96,64},{128,96},{160,128},{192,160},{224,192},{0,2... | collective-permute-start | bytes 36872 | tf_op jit(solution)/shard_map/ppermute | solution.py:477
  83.5 1.4 %collective-permute-done.24.from_up = f32[8,384]{1,0:T(8,128)S(1)} collective-permute-done((f32[8,384]{1,0:T(8,128)S(1)}, f32[8,384]{1,0:T(8,128)S(1)}, u32[]{:S(2)}, u32[]{:S(2)}) %collective-permute-start.24) | collective-permute-done | bytes 12320 | tf_op jit(solution)/shard_map/ppermute | solution.py:477
  84.9 2.1 %collective-permute-start.27 = (f32[8,384]{1,0:T(8,128)S(1)}, f32[8,384]{1,0:T(8,128)S(1)}, u32[]{:S(2)}, u32[]{:S(2)}) collective-permute-start(f32[8,384]{1,0:T(8,128)S(1)} %get-tuple-element.160), channel_id=1, source_target_pairs={{1,0},{2,1},{3,2},{4,3},{5,4},{6,5},{7,6},{8,7},{9,8},{10,9},{11,1... | collective-permute-start | bytes 36872 | tf_op jit(solution)/shard_map/ppermute | solution.py:470
  88.6 4.2 %collective-permute-done.26.from_left = f32[8,384]{1,0:T(8,128)S(1)} collective-permute-done((f32[8,384]{1,0:T(8,128)S(1)}, f32[8,384]{1,0:T(8,128)S(1)}, u32[]{:S(2)}, u32[]{:S(2)}) %collective-permute-start.26) | collective-permute-done | bytes 12320 | tf_op jit(solution)/shard_map/ppermute | solution.py:470
  93.4 2.9 %collective-permute-start.29 = (f32[8,384]{1,0:T(8,128)S(1)}, f32[8,384]{1,0:T(8,128)S(1)}, u32[]{:S(2)}, u32[]{:S(2)}) collective-permute-start(f32[8,384]{1,0:T(8,128)S(1)} %get-tuple-element.141), channel_id=1, source_target_pairs={{32,0},{64,32},{96,64},{128,96},{160,128},{192,160},{224,192},{0,2... | collective-permute-start | bytes 36872 | tf_op jit(solution)/shard_map/ppermute | solution.py:477
  96.3 1.2 %shard_map.144 = (f32[192,128]{1,0:T(8,128)S(1)}, f32[8,256]{1,0:T(8,128)S(1)}, f32[8,256]{1,0:T(8,128)S(1)}) custom-call(f32[8,128]{1,0:T(8,128)S(1)} %fusion.3.flags, f32[8,2048]{1,0:T(8,128)S(1)} %get-tuple-element.138.velocity, s32[128,128]{1,0:T(8,128)S(1)} %get-tuple-element.96.places, s32[16,128]{1,0:T(8,128)S(1)} %get-tuple-element.87.list_places), custom_call_target="tpu_custom_call" | custom-call | tf_op jit(solution)/shard_map/pallas_call | solution.py:452
  98.3 1.5 %collective-permute-start.30 = (f32[8,384]{1,0:T(8,128)S(1)}, f32[8,384]{1,0:T(8,128)S(1)}, u32[]{:S(2)}, u32[]{:S(2)}) collective-permute-start(f32[8,384]{1,0:T(8,128)S(1)} %get-tuple-element.159), channel_id=1, source_target_pairs={{0,1},{1,2},{2,3},{3,4},{4,5},{5,6},{6,7},{7,8},{8,9},{9,10},{10,1... | collective-permute-start | bytes 36872 | tf_op jit(solution)/shard_map/ppermute | solution.py:470
  99.8 1.4 %shard_map.145.far_ref = f32[192,128]{1,0:T(8,128)S(1)} custom-call(f32[8,128]{1,0:T(8,128)S(1)} %fusion.3.flags, f32[8,2048]{1,0:T(8,128)S(1)} %get-tuple-element.138.velocity, s32[128,128]{1,0:T(8,128)S(1)} %get-tuple-element.96.places, f32[8,384]{1,0:T(8,128)S(1)} %collective-permute-done.28.from_up, f32[8,384]{1,0:T(8,128)S(1)} %collective-permute-done.29.from_down), custom_call_target="tpu_custom_call" | custom-call | tf_op jit(solution)/shard_map/pallas_call | solution.py:452
  101.5 2.6 %collective-permute-done.30.from_left = f32[8,384]{1,0:T(8,128)S(1)} collective-permute-done((f32[8,384]{1,0:T(8,128)S(1)}, f32[8,384]{1,0:T(8,128)S(1)}, u32[]{:S(2)}, u32[]{:S(2)}) %collective-permute-start.30) | collective-permute-done | bytes 12320 | tf_op jit(solution)/shard_map/ppermute | solution.py:470
  104.1 1.3 %shard_map.146 = (f32[96,128]{1,0:T(8,128)}, f32[256,128]{1,0:T(8,128)S(1)}, f32[256,128]{1,0:T(8,128)S(1)}, f32[8,384]{1,0:T(8,128)S(1)}, f32[8,384]{1,0:T(8,12...) custom-call(f32[8,128]{1,0:T(8,128)S(1)} %fusion.3.flags, f32[192,128]{1,0:T(8,128)S(1)} %get-tuple-element.139.near_ref, ...), custom_call_target="tpu_custom_call" | custom-call | tf_op jit(solution)/shard_map/pallas_call | solution.py:452
  105.4 3.0 %collective-permute-start.33 = (f32[8,384]{1,0:T(8,128)S(1)}, f32[8,384]{1,0:T(8,128)S(1)}, u32[]{:S(2)}, u32[]{:S(2)}) collective-permute-start(f32[8,384]{1,0:T(8,128)S(1)} %get-tuple-element.148), channel_id=1, source_target_pairs={{32,0},{64,32},{96,64},{128,96},{160,128},{192,160},{224,192},{0,2... | collective-permute-start | bytes 36872 | tf_op jit(solution)/shard_map/ppermute | solution.py:477
  108.4 1.4 %collective-permute-done.32.from_up = f32[8,384]{1,0:T(8,128)S(1)} collective-permute-done((f32[8,384]{1,0:T(8,128)S(1)}, f32[8,384]{1,0:T(8,128)S(1)}, u32[]{:S(2)}, u32[]{:S(2)}) %collective-permute-start.32) | collective-permute-done | bytes 12320 | tf_op jit(solution)/shard_map/ppermute | solution.py:477
  109.8 2.1 %collective-permute-start.35 = (f32[8,384]{1,0:T(8,128)S(1)}, f32[8,384]{1,0:T(8,128)S(1)}, u32[]{:S(2)}, u32[]{:S(2)}) collective-permute-start(f32[8,384]{1,0:T(8,128)S(1)} %get-tuple-element.156), channel_id=1, source_target_pairs={{1,0},{2,1},{3,2},{4,3},{5,4},{6,5},{7,6},{8,7},{9,8},{10,9},{11,1... | collective-permute-start | bytes 36872 | tf_op jit(solution)/shard_map/ppermute | solution.py:470
  112.6 0.7 shard_map.148.own
  113.5 4.2 %collective-permute-done.34.from_left = f32[8,384]{1,0:T(8,128)S(1)} collective-permute-done((f32[8,384]{1,0:T(8,128)S(1)}, f32[8,384]{1,0:T(8,128)S(1)}, u32[]{:S(2)}, u32[]{:S(2)}) %collective-permute-start.34) | collective-permute-done | bytes 12320 | tf_op jit(solution)/shard_map/ppermute | solution.py:470
  117.7 0.9 shard_map.149
  (77 shorter events, 12.9 us)
Async XLA Ops:
  3.2 4.3 %collective-permute-start = (f32[8,384]{1,0:T(8,128)S(1)}, f32[8,384]{1,0:T(8,128)S(1)}, u32[]{:S(2)}, u32[]{:S(2)}) collective-permute-start(f32[8,384]{1,0:T(8,128)S(1)} %get-tuple-element.89), channel_id=1, source_target_pairs={{0,32},{32,64},{64,96},{96,128},{128,160},{160,192},{192,224},{224... | collective-permute-start | bytes 36872 | tf_op jit(solution)/shard_map/ppermute | solution.py:477
  3.2 4.3 %collective-permute-start.1 = (f32[8,384]{1,0:T(8,128)S(1)}, f32[8,384]{1,0:T(8,128)S(1)}, u32[]{:S(2)}, u32[]{:S(2)}) collective-permute-start(f32[8,384]{1,0:T(8,128)S(1)} %get-tuple-element.90), channel_id=1, source_target_pairs={{32,0},{64,32},{96,64},{128,96},{160,128},{192,160},{224,192},{0,2... | collective-permute-start | bytes 36872 | tf_op jit(solution)/shard_map/ppermute | solution.py:477
  7.6 8.4 %collective-permute-start.3 = (f32[8,384]{1,0:T(8,128)S(1)}, f32[8,384]{1,0:T(8,128)S(1)}, u32[]{:S(2)}, u32[]{:S(2)}) collective-permute-start(f32[8,384]{1,0:T(8,128)S(1)} %get-tuple-element.172), channel_id=1, source_target_pairs={{1,0},{2,1},{3,2},{4,3},{5,4},{6,5},{7,6},{8,7},{9,8},{10,9},{11,1... | collective-permute-start | bytes 36872 | tf_op jit(solution)/shard_map/ppermute | solution.py:470
  13.8 5.8 %collective-permute-start.2 = (f32[8,384]{1,0:T(8,128)S(1)}, f32[8,384]{1,0:T(8,128)S(1)}, u32[]{:S(2)}, u32[]{:S(2)}) collective-permute-start(f32[8,384]{1,0:T(8,128)S(1)} %get-tuple-element.173), channel_id=1, source_target_pairs={{0,1},{1,2},{2,3},{3,4},{4,5},{5,6},{6,7},{7,8},{8,9},{9,10},{10,1... | collective-permute-start | bytes 36872 | tf_op jit(solution)/shard_map/ppermute | solution.py:470
  20.0 4.3 %collective-permute-start.4 = (f32[8,384]{1,0:T(8,128)S(1)}, f32[8,384]{1,0:T(8,128)S(1)}, u32[]{:S(2)}, u32[]{:S(2)}) collective-permute-start(f32[8,384]{1,0:T(8,128)S(1)} %get-tuple-element.98), channel_id=1, source_target_pairs={{0,32},{32,64},{64,96},{96,128},{128,160},{160,192},{192,224},{224... | collective-permute-start | bytes 36872 | tf_op jit(solution)/shard_map/ppermute | solution.py:477
  20.1 4.3 %collective-permute-start.5 = (f32[8,384]{1,0:T(8,128)S(1)}, f32[8,384]{1,0:T(8,128)S(1)}, u32[]{:S(2)}, u32[]{:S(2)}) collective-permute-start(f32[8,384]{1,0:T(8,128)S(1)} %get-tuple-element.99), channel_id=1, source_target_pairs={{32,0},{64,32},{96,64},{128,96},{160,128},{192,160},{224,192},{0,2... | collective-permute-start | bytes 36872 | tf_op jit(solution)/shard_map/ppermute | solution.py:477
  24.4 3.7 %collective-permute-start.7 = (f32[8,384]{1,0:T(8,128)S(1)}, f32[8,384]{1,0:T(8,128)S(1)}, u32[]{:S(2)}, u32[]{:S(2)}) collective-permute-start(f32[8,384]{1,0:T(8,128)S(1)} %get-tuple-element.170), channel_id=1, source_target_pairs={{1,0},{2,1},{3,2},{4,3},{5,4},{6,5},{7,6},{8,7},{9,8},{10,9},{11,1... | collective-permute-start | bytes 36872 | tf_op jit(solution)/shard_map/ppermute | solution.py:470
  25.0 5.8 %collective-permute-start.6 = (f32[8,384]{1,0:T(8,128)S(1)}, f32[8,384]{1,0:T(8,128)S(1)}, u32[]{:S(2)}, u32[]{:S(2)}) collective-permute-start(f32[8,384]{1,0:T(8,128)S(1)} %get-tuple-element.171), channel_id=1, source_target_pairs={{0,1},{1,2},{2,3},{3,4},{4,5},{5,6},{6,7},{7,8},{8,9},{9,10},{10,1... | collective-permute-start | bytes 36872 | tf_op jit(solution)/shard_map/ppermute | solution.py:470
  31.7 4.3 %collective-permute-start.8 = (f32[8,384]{1,0:T(8,128)S(1)}, f32[8,384]{1,0:T(8,128)S(1)}, u32[]{:S(2)}, u32[]{:S(2)}) collective-permute-start(f32[8,384]{1,0:T(8,128)S(1)} %get-tuple-element.108), channel_id=1, source_target_pairs={{0,32},{32,64},{64,96},{96,128},{128,160},{160,192},{192,224},{224... | collective-permute-start | bytes 36872 | tf_op jit(solution)/shard_map/ppermute | solution.py:477
  31.7 4.3 %collective-permute-start.9 = (f32[8,384]{1,0:T(8,128)S(1)}, f32[8,384]{1,0:T(8,128)S(1)}, u32[]{:S(2)}, u32[]{:S(2)}) collective-permute-start(f32[8,384]{1,0:T(8,128)S(1)} %get-tuple-element.109), channel_id=1, source_target_pairs={{32,0},{64,32},{96,64},{128,96},{160,128},{192,160},{224,192},{0,2... | collective-permute-start | bytes 36872 | tf_op jit(solution)/shard_map/ppermute | solution.py:477
  36.0 3.7 %collective-permute-start.11 = (f32[8,384]{1,0:T(8,128)S(1)}, f32[8,384]{1,0:T(8,128)S(1)}, u32[]{:S(2)}, u32[]{:S(2)}) collective-permute-start(f32[8,384]{1,0:T(8,128)S(1)} %get-tuple-element.168), channel_id=1, source_target_pairs={{1,0},{2,1},{3,2},{4,3},{5,4},{6,5},{7,6},{8,7},{9,8},{10,9},{11,1... | collective-permute-start | bytes 36872 | tf_op jit(solution)/shard_map/ppermute | solution.py:470
  38.2 5.8 %collective-permute-start.10 = (f32[8,384]{1,0:T(8,128)S(1)}, f32[8,384]{1,0:T(8,128)S(1)}, u32[]{:S(2)}, u32[]{:S(2)}) collective-permute-start(f32[8,384]{1,0:T(8,128)S(1)} %get-tuple-element.169), channel_id=1, source_target_pairs={{0,1},{1,2},{2,3},{3,4},{4,5},{5,6},{6,7},{7,8},{8,9},{9,10},{10,1... | collective-permute-start | bytes 36872 | tf_op jit(solution)/shard_map/ppermute | solution.py:470
  44.5 4.3 %collective-permute-start.12 = (f32[8,384]{1,0:T(8,128)S(1)}, f32[8,384]{1,0:T(8,128)S(1)}, u32[]{:S(2)}, u32[]{:S(2)}) collective-permute-start(f32[8,384]{1,0:T(8,128)S(1)} %get-tuple-element.114), channel_id=1, source_target_pairs={{0,32},{32,64},{64,96},{96,128},{128,160},{160,192},{192,224},{224... | collective-permute-start | bytes 36872 | tf_op jit(solution)/shard_map/ppermute | solution.py:477
  44.5 4.3 %collective-permute-start.13 = (f32[8,384]{1,0:T(8,128)S(1)}, f32[8,384]{1,0:T(8,128)S(1)}, u32[]{:S(2)}, u32[]{:S(2)}) collective-permute-start(f32[8,384]{1,0:T(8,128)S(1)} %get-tuple-element.115), channel_id=1, source_target_pairs={{32,0},{64,32},{96,64},{128,96},{160,128},{192,160},{224,192},{0,2... | collective-permute-start | bytes 36872 | tf_op jit(solution)/shard_map/ppermute | solution.py:477
  48.9 3.7 %collective-permute-start.15 = (f32[8,384]{1,0:T(8,128)S(1)}, f32[8,384]{1,0:T(8,128)S(1)}, u32[]{:S(2)}, u32[]{:S(2)}) collective-permute-start(f32[8,384]{1,0:T(8,128)S(1)} %get-tuple-element.166), channel_id=1, source_target_pairs={{1,0},{2,1},{3,2},{4,3},{5,4},{6,5},{7,6},{8,7},{9,8},{10,9},{11,1... | collective-permute-start | bytes 36872 | tf_op jit(solution)/shard_map/ppermute | solution.py:470
  49.4 5.8 %collective-permute-start.14 = (f32[8,384]{1,0:T(8,128)S(1)}, f32[8,384]{1,0:T(8,128)S(1)}, u32[]{:S(2)}, u32[]{:S(2)}) collective-permute-start(f32[8,384]{1,0:T(8,128)S(1)} %get-tuple-element.167), channel_id=1, source_target_pairs={{0,1},{1,2},{2,3},{3,4},{4,5},{5,6},{6,7},{7,8},{8,9},{9,10},{10,1... | collective-permute-start | bytes 36872 | tf_op jit(solution)/shard_map/ppermute | solution.py:470
  56.1 4.3 %collective-permute-start.16 = (f32[8,384]{1,0:T(8,128)S(1)}, f32[8,384]{1,0:T(8,128)S(1)}, u32[]{:S(2)}, u32[]{:S(2)}) collective-permute-start(f32[8,384]{1,0:T(8,128)S(1)} %get-tuple-element.121), channel_id=1, source_target_pairs={{0,32},{32,64},{64,96},{96,128},{128,160},{160,192},{192,224},{224... | collective-permute-start | bytes 36872 | tf_op jit(solution)/shard_map/ppermute | solution.py:477
  56.1 4.3 %collective-permute-start.17 = (f32[8,384]{1,0:T(8,128)S(1)}, f32[8,384]{1,0:T(8,128)S(1)}, u32[]{:S(2)}, u32[]{:S(2)}) collective-permute-start(f32[8,384]{1,0:T(8,128)S(1)} %get-tuple-element.122), channel_id=1, source_target_pairs={{32,0},{64,32},{96,64},{128,96},{160,128},{192,160},{224,192},{0,2... | collective-permute-start | bytes 36872 | tf_op jit(solution)/shard_map/ppermute | solution.py:477
  60.5 3.7 %collective-permute-start.19 = (f32[8,384]{1,0:T(8,128)S(1)}, f32[8,384]{1,0:T(8,128)S(1)}, u32[]{:S(2)}, u32[]{:S(2)}) collective-permute-start(f32[8,384]{1,0:T(8,128)S(1)} %get-tuple-element.164), channel_id=1, source_target_pairs={{1,0},{2,1},{3,2},{4,3},{5,4},{6,5},{7,6},{8,7},{9,8},{10,9},{11,1... | collective-permute-start | bytes 36872 | tf_op jit(solution)/shard_map/ppermute | solution.py:470
  62.6 5.8 %collective-permute-start.18 = (f32[8,384]{1,0:T(8,128)S(1)}, f32[8,384]{1,0:T(8,128)S(1)}, u32[]{:S(2)}, u32[]{:S(2)}) collective-permute-start(f32[8,384]{1,0:T(8,128)S(1)} %get-tuple-element.165), channel_id=1, source_target_pairs={{0,1},{1,2},{2,3},{3,4},{4,5},{5,6},{6,7},{7,8},{8,9},{9,10},{10,1... | collective-permute-start | bytes 36872 | tf_op jit(solution)/shard_map/ppermute | solution.py:470
  68.9 4.3 %collective-permute-start.20 = (f32[8,384]{1,0:T(8,128)S(1)}, f32[8,384]{1,0:T(8,128)S(1)}, u32[]{:S(2)}, u32[]{:S(2)}) collective-permute-start(f32[8,384]{1,0:T(8,128)S(1)} %get-tuple-element.127), channel_id=1, source_target_pairs={{0,32},{32,64},{64,96},{96,128},{128,160},{160,192},{192,224},{224... | collective-permute-start | bytes 36872 | tf_op jit(solution)/shard_map/ppermute | solution.py:477
  68.9 4.3 %collective-permute-start.21 = (f32[8,384]{1,0:T(8,128)S(1)}, f32[8,384]{1,0:T(8,128)S(1)}, u32[]{:S(2)}, u32[]{:S(2)}) collective-permute-start(f32[8,384]{1,0:T(8,128)S(1)} %get-tuple-element.128), channel_id=1, source_target_pairs={{32,0},{64,32},{96,64},{128,96},{160,128},{192,160},{224,192},{0,2... | collective-permute-start | bytes 36872 | tf_op jit(solution)/shard_map/ppermute | solution.py:477
  73.3 3.7 %collective-permute-start.23 = (f32[8,384]{1,0:T(8,128)S(1)}, f32[8,384]{1,0:T(8,128)S(1)}, u32[]{:S(2)}, u32[]{:S(2)}) collective-permute-start(f32[8,384]{1,0:T(8,128)S(1)} %get-tuple-element.162), channel_id=1, source_target_pairs={{1,0},{2,1},{3,2},{4,3},{5,4},{6,5},{7,6},{8,7},{9,8},{10,9},{11,1... | collective-permute-start | bytes 36872 | tf_op jit(solution)/shard_map/ppermute | solution.py:470
  73.9 5.8 %collective-permute-start.22 = (f32[8,384]{1,0:T(8,128)S(1)}, f32[8,384]{1,0:T(8,128)S(1)}, u32[]{:S(2)}, u32[]{:S(2)}) collective-permute-start(f32[8,384]{1,0:T(8,128)S(1)} %get-tuple-element.163), channel_id=1, source_target_pairs={{0,1},{1,2},{2,3},{3,4},{4,5},{5,6},{6,7},{7,8},{8,9},{9,10},{10,1... | collective-permute-start | bytes 36872 | tf_op jit(solution)/shard_map/ppermute | solution.py:470
  80.5 4.3 %collective-permute-start.24 = (f32[8,384]{1,0:T(8,128)S(1)}, f32[8,384]{1,0:T(8,128)S(1)}, u32[]{:S(2)}, u32[]{:S(2)}) collective-permute-start(f32[8,384]{1,0:T(8,128)S(1)} %get-tuple-element.134), channel_id=1, source_target_pairs={{0,32},{32,64},{64,96},{96,128},{128,160},{160,192},{192,224},{224... | collective-permute-start | bytes 36872 | tf_op jit(solution)/shard_map/ppermute | solution.py:477
  80.5 4.3 %collective-permute-start.25 = (f32[8,384]{1,0:T(8,128)S(1)}, f32[8,384]{1,0:T(8,128)S(1)}, u32[]{:S(2)}, u32[]{:S(2)}) collective-permute-start(f32[8,384]{1,0:T(8,128)S(1)} %get-tuple-element.135), channel_id=1, source_target_pairs={{32,0},{64,32},{96,64},{128,96},{160,128},{192,160},{224,192},{0,2... | collective-permute-start | bytes 36872 | tf_op jit(solution)/shard_map/ppermute | solution.py:477
  84.9 3.7 %collective-permute-start.27 = (f32[8,384]{1,0:T(8,128)S(1)}, f32[8,384]{1,0:T(8,128)S(1)}, u32[]{:S(2)}, u32[]{:S(2)}) collective-permute-start(f32[8,384]{1,0:T(8,128)S(1)} %get-tuple-element.160), channel_id=1, source_target_pairs={{1,0},{2,1},{3,2},{4,3},{5,4},{6,5},{7,6},{8,7},{9,8},{10,9},{11,1... | collective-permute-start | bytes 36872 | tf_op jit(solution)/shard_map/ppermute | solution.py:470
  87.0 5.8 %collective-permute-start.26 = (f32[8,384]{1,0:T(8,128)S(1)}, f32[8,384]{1,0:T(8,128)S(1)}, u32[]{:S(2)}, u32[]{:S(2)}) collective-permute-start(f32[8,384]{1,0:T(8,128)S(1)} %get-tuple-element.161), channel_id=1, source_target_pairs={{0,1},{1,2},{2,3},{3,4},{4,5},{5,6},{6,7},{7,8},{8,9},{9,10},{10,1... | collective-permute-start | bytes 36872 | tf_op jit(solution)/shard_map/ppermute | solution.py:470
  93.3 4.3 %collective-permute-start.28 = (f32[8,384]{1,0:T(8,128)S(1)}, f32[8,384]{1,0:T(8,128)S(1)}, u32[]{:S(2)}, u32[]{:S(2)}) collective-permute-start(f32[8,384]{1,0:T(8,128)S(1)} %get-tuple-element.140), channel_id=1, source_target_pairs={{0,32},{32,64},{64,96},{96,128},{128,160},{160,192},{192,224},{224... | collective-permute-start | bytes 36872 | tf_op jit(solution)/shard_map/ppermute | solution.py:477
  93.4 4.3 %collective-permute-start.29 = (f32[8,384]{1,0:T(8,128)S(1)}, f32[8,384]{1,0:T(8,128)S(1)}, u32[]{:S(2)}, u32[]{:S(2)}) collective-permute-start(f32[8,384]{1,0:T(8,128)S(1)} %get-tuple-element.141), channel_id=1, source_target_pairs={{32,0},{64,32},{96,64},{128,96},{160,128},{192,160},{224,192},{0,2... | collective-permute-start | bytes 36872 | tf_op jit(solution)/shard_map/ppermute | solution.py:477
  97.7 3.7 %collective-permute-start.31 = (f32[8,384]{1,0:T(8,128)S(1)}, f32[8,384]{1,0:T(8,128)S(1)}, u32[]{:S(2)}, u32[]{:S(2)}) collective-permute-start(f32[8,384]{1,0:T(8,128)S(1)} %get-tuple-element.158), channel_id=1, source_target_pairs={{1,0},{2,1},{3,2},{4,3},{5,4},{6,5},{7,6},{8,7},{9,8},{10,9},{11,1... | collective-permute-start | bytes 36872 | tf_op jit(solution)/shard_map/ppermute | solution.py:470
  98.3 5.8 %collective-permute-start.30 = (f32[8,384]{1,0:T(8,128)S(1)}, f32[8,384]{1,0:T(8,128)S(1)}, u32[]{:S(2)}, u32[]{:S(2)}) collective-permute-start(f32[8,384]{1,0:T(8,128)S(1)} %get-tuple-element.159), channel_id=1, source_target_pairs={{0,1},{1,2},{2,3},{3,4},{4,5},{5,6},{6,7},{7,8},{8,9},{9,10},{10,1... | collective-permute-start | bytes 36872 | tf_op jit(solution)/shard_map/ppermute | solution.py:470
  105.4 4.3 %collective-permute-start.32 = (f32[8,384]{1,0:T(8,128)S(1)}, f32[8,384]{1,0:T(8,128)S(1)}, u32[]{:S(2)}, u32[]{:S(2)}) collective-permute-start(f32[8,384]{1,0:T(8,128)S(1)} %get-tuple-element.147), channel_id=1, source_target_pairs={{0,32},{32,64},{64,96},{96,128},{128,160},{160,192},{192,224},{224... | collective-permute-start | bytes 36872 | tf_op jit(solution)/shard_map/ppermute | solution.py:477
  105.4 4.4 %collective-permute-start.33 = (f32[8,384]{1,0:T(8,128)S(1)}, f32[8,384]{1,0:T(8,128)S(1)}, u32[]{:S(2)}, u32[]{:S(2)}) collective-permute-start(f32[8,384]{1,0:T(8,128)S(1)} %get-tuple-element.148), channel_id=1, source_target_pairs={{32,0},{64,32},{96,64},{128,96},{160,128},{192,160},{224,192},{0,2... | collective-permute-start | bytes 36872 | tf_op jit(solution)/shard_map/ppermute | solution.py:477
  109.8 3.7 %collective-permute-start.35 = (f32[8,384]{1,0:T(8,128)S(1)}, f32[8,384]{1,0:T(8,128)S(1)}, u32[]{:S(2)}, u32[]{:S(2)}) collective-permute-start(f32[8,384]{1,0:T(8,128)S(1)} %get-tuple-element.156), channel_id=1, source_target_pairs={{1,0},{2,1},{3,2},{4,3},{5,4},{6,5},{7,6},{8,7},{9,8},{10,9},{11,1... | collective-permute-start | bytes 36872 | tf_op jit(solution)/shard_map/ppermute | solution.py:470
  111.9 5.8 %collective-permute-start.34 = (f32[8,384]{1,0:T(8,128)S(1)}, f32[8,384]{1,0:T(8,128)S(1)}, u32[]{:S(2)}, u32[]{:S(2)}) collective-permute-start(f32[8,384]{1,0:T(8,128)S(1)} %get-tuple-element.157), channel_id=1, source_target_pairs={{0,1},{1,2},{2,3},{3,4},{4,5},{5,6},{6,7},{7,8},{8,9},{9,10},{10,1... | collective-permute-start | bytes 36872 | tf_op jit(solution)/shard_map/ppermute | solution.py:470
where the time goes:
time: 119 us
  starting transfers between devices  49.7 us (42%)
  waiting for transfers between devices  40.4 us (34%)
  Pallas kernels  27.3 us (23%)
    ppermute x18, waiting for transfers between devices, loop(): return lax.ppermute(value, ('gx', 'gy'), pairs)  32.7 us
    pallas_call x28, Pallas kernels, call(): pl.pallas_call(body, out_shape=outs, in_specs=specs or [vmem] * len(opera...  27.3 us
    ppermute x18, starting transfers between devices, along_gx(): return (lax.ppermute(first, 'gx', down), lax.ppermute(second, 'gx', up))  26.6 us
    ppermute x18, starting transfers between devices, loop(): return lax.ppermute(value, ('gx', 'gy'), pairs)  23.1 us
    ppermute x18, waiting for transfers between devices, along_gx(): return (lax.ppermute(first, 'gx', down), lax.ppermute(second, 'gx', up))  7.72 us
  transfers between devices with their start and end apart: 36, of which 26 were waited for; matrix products, arithmetic and copies ran while one was open for 0% of the time, Pallas kernels for 16%

commit v1 on v0

--- a/solution.py
+++ b/solution.py
@@ -19,7 +19,6 @@
 OWN_TILES = BODY // 128
 WIDE = 256
 OWN_WIDE = BODY // WIDE
-GHOST_WIDE = 6
 IMPULSE_ROWS = 3 * ROWS
 MESSAGE = FACE + 128
 
@@ -78,7 +77,8 @@
 
 
 OWN_BLOCKS = tuple(range(OWN_WIDE))
-GHOST_BLOCKS = tuple(range(OWN_WIDE, OWN_WIDE + GHOST_WIDE))
+GX_BLOCKS = (OWN_WIDE, OWN_WIDE + 1, OWN_WIDE + 4, OWN_WIDE + 5)
+GY_BLOCKS = (OWN_WIDE + 2, OWN_WIDE + 3)
 
 
 def lane_hot(ref, low, rows):
@@ -94,7 +94,7 @@
     return total[:blocks * 8] + total[blocks * 8:]
 
 
-def end_pulses(impulse, table, near_out, far_out):
+def end_pulses(impulse, table, out, arm, sign):
     p0, p1, p2 = impulse
     get = lambda name: plane(table, PLANE[name])
     a0, a1 = get("a0"), get("a1")
@@ -105,15 +105,12 @@
         p0 * get("n2") + p2 * b2,
     )
     twist = (p1 * b0 - p2 * a0, p1 * b1 - p2 * a1, p1 * b2)
-    arm0, arm1 = -get("arm0"), -get("arm1")
+    arm = -get(arm)
     for comp in range(3):
-        near_out[pl.ds(comp, ROWS, stride=8), :] = force[comp]
-        far_out[pl.ds(comp, ROWS, stride=8), :] = -force[comp]
-        near_out[pl.ds(comp + 3, ROWS, stride=8), :] = arm0 * twist[comp]
-        far_out[pl.ds(comp + 3, ROWS, stride=8), :] = arm1 * twist[comp]
+        out[pl.ds(comp, ROWS, stride=8), :] = sign * force[comp]
+        out[pl.ds(comp + 3, ROWS, stride=8), :] = arm * twist[comp]
     for comp in (6, 7):
-        near_out[pl.ds(comp, ROWS, stride=8), :] = jnp.zeros((ROWS, 128), F32)
-        far_out[pl.ds(comp, ROWS, stride=8), :] = jnp.zeros((ROWS, 128), F32)
+        out[pl.ds(comp, ROWS, stride=8), :] = jnp.zeros((ROWS, 128), F32)
 
 
 def spread_rows(left, values, high, blocks):
@@ -122,12 +119,16 @@
         spread(left, high[row:row + 1, :], halves(value), blocks, row * 128)
 
 
-def ghost_pulses(flags, far, high_far, hot_far, gx_sends, gy_faces, left_ghost):
-    spread_rows(left_ghost, far, high_far, GHOST_BLOCKS)
-    total = product(left_ghost, hot_far[...], GHOST_WIDE)
-    ghost = [total[block * 8:block * 8 + 8] for block in range(5)]
-    send_gx(flags, ghost[0], ghost[1], ghost[4][:, :128], gx_sends)
-    send_gy(flags, ghost[2], ghost[3], gy_faces)
+def ghost_pulses(flags, far, high_far, hot_far, gx_sends, left_ghost):
+    spread_rows(left_ghost, far, high_far, GX_BLOCKS)
+    total = product(left_ghost, hot_far[...], len(GX_BLOCKS))
+    send_gx(flags, total[:8], total[8:16], total[16:24, :128], gx_sends)
+
+
+def ghost_faces(flags, far, high_far, hot_far, gy_faces, left_gy):
+    spread_rows(left_gy, far, high_far, GY_BLOCKS)
+    total = product(left_gy, hot_far[...], len(GY_BLOCKS))
+    send_gy(flags, total[:8], total[8:], gy_faces)
 
 
 def flag(flags, number, width=128):
@@ -155,8 +156,8 @@
 def prepare(
     flags, angles_in, arms_in, mu_in, bias_in, impulse_in, owner_in, other_in,
     radius_in, faces_in, corners_in, base_in,
-    table, places, high_far, impulse, hot_far, near_values, far_values,
-    gx_first, gx_second, gy_first, gy_second,
+    table, places, high_far, impulse, hot_far, far_values,
+    gx_first, gx_second,
     owner, radius, faces, corners, base,
     angles, arms, mu, bias, other, flat, left_ghost, sems,
 ):
@@ -209,17 +210,16 @@
     for name, value in values.items():
         number = PLANE[name]
         table[number * ROWS:(number + 1) * ROWS, :] = value
-    end_pulses([plane(impulse, comp) for comp in range(3)], table, near_values, far_values)
-    ghost_pulses(
-        flags, far_values, high_far, hot_far, (gx_first, gx_second), (gy_first, gy_second), left_ghost
-    )
+    end_pulses([plane(impulse, comp) for comp in range(3)], table, far_values, "arm1", -1.0)
+    ghost_pulses(flags, far_values, high_far, hot_far, (gx_first, gx_second), left_ghost)
 
 
 def prepare_own(
-    near_values, owner, radius, faces, corners, base_rows,
-    pulse, high_near, hot_near, hot_list, list_places, inverse, base,
-    left_near,
-):
+    flags, far_values, high_far, hot_far, impulse, table, owner, radius, faces, corners, base_rows,
+    gy_first, gy_second, pulse, high_near, hot_near, hot_list, list_places, inverse, base,
+    near_values, left_near, left_gy,
+):
+    ghost_faces(flags, far_values, high_far, hot_far, (gy_first, gy_second), left_gy)
     near_id = owner[...]
     high_near[...] = near_id >> 8
     lane_hot(hot_near, near_id & 255, ROWS)
@@ -241,7 +241,7 @@
     inverse[...] = jnp.where(iota((8, BODY), 0) < 3, linear, angular)
     for tile in range(OWN_TILES):
         base[:, tile * 128:(tile + 1) * 128] = base_rows[pl.ds(tile, 6, stride=OWN_TILES), :]
-    scatter_near(near_values, high_near, hot_near, pulse, left_near)
+    near_pulses(impulse, table, high_near, hot_near, pulse, near_values, left_near)
 
 
 def store_blocks(pulse, total):
@@ -249,9 +249,18 @@
         pulse[:, block * WIDE:(block + 1) * WIDE] = total[block * 8:block * 8 + 8]
 
 
-def scatter_near(values, high_near, hot_near, pulse, left_near):
+def near_pulses(impulse, table, high_near, hot_near, pulse, values, left_near):
+    end_pulses([plane(impulse, comp) for comp in range(3)], table, values, "arm0", 1.0)
     spread_rows(left_near, values, high_near, OWN_BLOCKS)
     store_blocks(pulse, product(left_near, hot_near[...], OWN_WIDE))
+
+
+def scatter_near(
+    flags, far_values, high_far, hot_far, impulse, table, high_near, hot_near,
+    gy_first, gy_second, pulse, near_values, left_near, left_gy,
+):
+    ghost_faces(flags, far_values, high_far, hot_far, (gy_first, gy_second), left_gy)
+    near_pulses(impulse, table, high_near, hot_near, pulse, near_values, left_near)
 
 
 def masked(flags, number, value):
@@ -393,7 +402,7 @@
 
 def sweep(
     flags, near_ref, far_ref, table, places, high_far, hot_far, impulse, from_left, from_right,
-    impulse_out, near_values, far_values, gx_first, gx_second, gy_first, gy_second, left_ghost,
+    impulse_out, far_values, gx_first, gx_second, left_ghost,
 ):
     near = [plane(near_ref, comp) for comp in range(6)]
     far = pick(
@@ -425,10 +434,8 @@
     ]
     for comp in range(3):
         impulse_out[comp * ROWS:(comp + 1) * ROWS, :] = fresh[comp]
-    end_pulses(fresh, table, near_values, far_values)
-    ghost_pulses(
-        flags, far_values, high_far, hot_far, (gx_first, gx_second), (gy_first, gy_second), left_ghost
-    )
+    end_pulses(fresh, table, far_values, "arm1", -1.0)
+    ghost_pulses(flags, far_values, high_far, hot_far, (gx_first, gx_second), left_ghost)
 
 
 def shape(*dims, kind=F32):
@@ -440,7 +447,10 @@
 VALUES = shape(8 * ROWS, 128)
 PULSE = shape(8, BODY)
 LEFT_OWN = pltpu.VMEM((2 * OWN_WIDE * 8, CONTACTS), BF16)
-LEFT_GHOST = pltpu.VMEM((2 * GHOST_WIDE * 8, CONTACTS), BF16)
+LEFT_GHOST = pltpu.VMEM((2 * len(GX_BLOCKS) * 8, CONTACTS), BF16)
+NEAR = (
+    pltpu.VMEM((8 * ROWS, 128), F32), LEFT_OWN, pltpu.VMEM((2 * len(GY_BLOCKS) * 8, CONTACTS), BF16)
+)
 
 
 def left_list(tiles):
@@ -521,8 +531,8 @@
         )
     ]
     (
-        table, places, high_far, impulse, hot_far, near_values, far_values,
-        gx_first, gx_second, gy_first, gy_second, owner, radius, faces, corners, base_rows,
+        table, places, high_far, impulse, hot_far, far_values,
+        gx_first, gx_second, owner, radius, faces, corners, base_rows,
     ) = call(
         prepare,
         (
@@ -531,8 +541,8 @@
             shape(ROWS, 128, kind=I32),
             shape(IMPULSE_ROWS, 128),
             shape(CONTACTS, WIDE, kind=BF16),
-            VALUES, VALUES,
-        ) + GX_SENDS + FACES + (
+            VALUES,
+        ) + GX_SENDS + (
             shape(ROWS, 128, kind=I32),
             shape(1, BODY),
             shape(4, FACE, kind=I32),
@@ -556,9 +566,9 @@
     for number in range(SWEEPS + 1):
         got = along_gx(gx_first, gx_second)
         if number == 0:
-            pulse, high_near, hot_near, hot_list, list_places, inverse, base = call(
+            gy_first, gy_second, pulse, high_near, hot_near, hot_list, list_places, inverse, base = call(
                 prepare_own,
-                (
+                FACES + (
                     PULSE,
                     shape(ROWS, 128, kind=I32),
                     shape(CONTACTS, WIDE, kind=BF16),
@@ -567,12 +577,14 @@
                     PULSE,
                     shape(6, BODY),
                 ),
-                (LEFT_OWN,),
-                near_values, owner, radius, faces, corners, base_rows,
+                NEAR,
+                flags, far_values, high_far, hot_far, impulse, table,
+                owner, radius, faces, corners, base_rows,
             )
         else:
-            (pulse,) = call(
-                scatter_near, (PULSE,), (LEFT_OWN,), near_values, high_near, hot_near
+            gy_first, gy_second, pulse = call(
+                scatter_near, FACES + (PULSE,), NEAR,
+                flags, far_values, high_far, hot_far, impulse, table, high_near, hot_near,
             )
         got_gy = along_gy(*got, gy_first, gy_second)
         (own,) = call(
@@ -596,8 +608,8 @@
         (far,) = call(
             gather_far, (shape(6 * ROWS, 128),), (), flags, velocity, places, *got
         )
-        impulse, near_values, far_values, gx_first, gx_second, gy_first, gy_second = call(
-            sweep, (shape(IMPULSE_ROWS, 128), VALUES, VALUES) + GX_SENDS + FACES, (LEFT_GHOST,),
+        impulse, far_values, gx_first, gx_second = call(
+            sweep, (shape(IMPULSE_ROWS, 128), VALUES) + GX_SENDS, (LEFT_GHOST,),
             flags, near, far, table, places, high_far, hot_far, impulse, *got_gy,
         )
     return velocity.reshape(1, 1, 6, BODY), impulse.reshape(1, 1, 3, CONTACTS)

time: 119 us -> 119 us (level)
  waiting for transfers between devices: 40.4 us -> 37.4 us
  starting transfers between devices: 49.7 us -> 51.7 us
    ppermute x18, waiting for transfers between devices: 7.72 us -> 2.14 us  [along_gx(): return (lax.ppermute(first, 'gx', down), lax.ppermute(second, 'gx', up))]
    ppermute x18, waiting for transfers between devices: 32.7 us -> 35.2 us  [loop(): return lax.ppermute(value, ('gx', 'gy'), pairs)]
    ppermute x18, starting transfers between devices: 23.1 us -> 25.1 us  [loop(): return lax.ppermute(value, ('gx', 'gy'), pairs)]
  transfers between devices with their start and end apart: 36 -> 36, of which waited for: 26 -> 25; matrix products, arithmetic and copies ran while one was open for 0% -> 0% of each run, Pallas kernels for 16% -> 16%
where the time goes in v1:
time: 119 us
  starting transfers between devices  51.7 us (43%)
  waiting for transfers between devices  37.4 us (31%)
  Pallas kernels  27.9 us (23%)
    ppermute x18, waiting for transfers between devices, loop(): return lax.ppermute(value, ('gx', 'gy'), pairs)  35.2 us
    pallas_call x28, Pallas kernels, call(): pl.pallas_call(body, out_shape=outs, in_specs=specs or [vmem] * len(opera...  27.9 us
    ppermute x18, starting transfers between devices, along_gx(): return (lax.ppermute(first, 'gx', down), lax.ppermute(second, 'gx', up))  26.7 us
    ppermute x18, starting transfers between devices, loop(): return lax.ppermute(value, ('gx', 'gy'), pairs)  25.1 us
  transfers between devices with their start and end apart: 36, of which 25 were waited for; matrix products, arithmetic and copies ran while one was open for 0% of the time, Pallas kernels for 16%

profile of v1, /device:TPU:6, one launch (start us, length us, event | category | flops | bytes accessed | tf_op | source)
XLA Modules:
  0.0 118.9 jit_solution(4316242562509556852)
XLA Ops:
  0.8 2.3 %shard_map.122 = (f32[416,128]{1,0:T(8,128)S(1)}, s32[128,128]{1,0:T(8,128)S(1)}, s32[32,128]{1,0:T(8,128)S(1)}, f32[96,128]{1,0:T(8,128)S(1)}, bf16[4096,256]{1...) custom-call(f32[8,128]{1,0:T(8,128)S(1)} %fusion.3.flags, ...), custom_call_target="tpu_custom_call" | custom-call | tf_op jit(solution)/shard_map/pallas_call | solution.py:462
  3.1 2.9 %collective-permute-start.1 = (f32[8,384]{1,0:T(8,128)S(1)}, f32[8,384]{1,0:T(8,128)S(1)}, u32[]{:S(2)}, u32[]{:S(2)}) collective-permute-start(f32[8,384]{1,0:T(8,128)S(1)} %get-tuple-element.90), channel_id=1, source_target_pairs={{32,0},{64,32},{96,64},{128,96},{160,128},{192,160},{224,192},{0,2... | collective-permute-start | bytes 36872 | tf_op jit(solution)/shard_map/ppermute | solution.py:487
  6.1 1.6 %shard_map.123 = (f32[8,256]{1,0:T(8,128)S(1)}, f32[8,256]{1,0:T(8,128)S(1)}, f32[8,2048]{1,0:T(8,128)S(1)}, s32[32,128]{1,0:T(8,128)S(1)}, bf16[4096,256]{1,0:T...) custom-call(f32[8,128]{1,0:T(8,128)S(1)} %fusion.3.flags, ...), custom_call_target="tpu_custom_call" | custom-call | tf_op jit(solution)/shard_map/pallas_call | solution.py:462
  7.8 6.2 %collective-permute-start.3 = (f32[8,384]{1,0:T(8,128)S(1)}, f32[8,384]{1,0:T(8,128)S(1)}, u32[]{:S(2)}, u32[]{:S(2)}) collective-permute-start(f32[8,384]{1,0:T(8,128)S(1)} %get-tuple-element.170), channel_id=1, source_target_pairs={{1,0},{2,1},{3,2},{4,3},{5,4},{6,5},{7,6},{8,7},{9,8},{10,9},{11,1... | collective-permute-start | bytes 36872 | tf_op jit(solution)/shard_map/ppermute | solution.py:480
  15.4 4.4 %collective-permute-done.2.from_left = f32[8,384]{1,0:T(8,128)S(1)} collective-permute-done((f32[8,384]{1,0:T(8,128)S(1)}, f32[8,384]{1,0:T(8,128)S(1)}, u32[]{:S(2)}, u32[]{:S(2)}) %collective-permute-start.2) | collective-permute-done | bytes 12320 | tf_op jit(solution)/shard_map/ppermute | solution.py:480
  20.3 2.9 %collective-permute-start.5 = (f32[8,384]{1,0:T(8,128)S(1)}, f32[8,384]{1,0:T(8,128)S(1)}, u32[]{:S(2)}, u32[]{:S(2)}) collective-permute-start(f32[8,384]{1,0:T(8,128)S(1)} %get-tuple-element.99), channel_id=1, source_target_pairs={{32,0},{64,32},{96,64},{128,96},{160,128},{192,160},{224,192},{0,2... | collective-permute-start | bytes 36872 | tf_op jit(solution)/shard_map/ppermute | solution.py:487
  23.2 1.2 %shard_map.126 = (f32[192,128]{1,0:T(8,128)S(1)}, f32[8,256]{1,0:T(8,128)S(1)}, f32[8,256]{1,0:T(8,128)S(1)}) custom-call(f32[8,128]{1,0:T(8,128)S(1)} %fusion.3.flags, f32[8,2048]{1,0:T(8,128)S(1)} %get-tuple-element.95.velocity, s32[128,128]{1,0:T(8,128)S(1)} %get-tuple-element.96.places, s32[16,128]{1,0:T(8,128)S(1)} %get-tuple-element.87.list_places), custom_call_target="tpu_custom_call" | custom-call | tf_op jit(solution)/shard_map/pallas_call | solution.py:462
  24.7 2.0 %collective-permute-start.6 = (f32[8,384]{1,0:T(8,128)S(1)}, f32[8,384]{1,0:T(8,128)S(1)}, u32[]{:S(2)}, u32[]{:S(2)}) collective-permute-start(f32[8,384]{1,0:T(8,128)S(1)} %get-tuple-element.169), channel_id=1, source_target_pairs={{0,1},{1,2},{2,3},{3,4},{4,5},{5,6},{6,7},{7,8},{8,9},{9,10},{10,1... | collective-permute-start | bytes 36872 | tf_op jit(solution)/shard_map/ppermute | solution.py:480
  26.7 1.4 %shard_map.127.far_ref = f32[192,128]{1,0:T(8,128)S(1)} custom-call(f32[8,128]{1,0:T(8,128)S(1)} %fusion.3.flags, f32[8,2048]{1,0:T(8,128)S(1)} %get-tuple-element.95.velocity, s32[128,128]{1,0:T(8,128)S(1)} %get-tuple-element.96.places, f32[8,384]{1,0:T(8,128)S(1)} %collective-permute-done.4.from_up, f32[8,384]{1,0:T(8,128)S(1)} %collective-permute-done.5.from_down), custom_call_target="tpu_custom_call" | custom-call | tf_op jit(solution)/shard_map/pallas_call | solution.py:462
  28.4 2.2 %collective-permute-done.6.from_left = f32[8,384]{1,0:T(8,128)S(1)} collective-permute-done((f32[8,384]{1,0:T(8,128)S(1)}, f32[8,384]{1,0:T(8,128)S(1)}, u32[]{:S(2)}, u32[]{:S(2)}) %collective-permute-start.6) | collective-permute-done | bytes 12320 | tf_op jit(solution)/shard_map/ppermute | solution.py:480
  31.3 3.0 %collective-permute-start.9 = (f32[8,384]{1,0:T(8,128)S(1)}, f32[8,384]{1,0:T(8,128)S(1)}, u32[]{:S(2)}, u32[]{:S(2)}) collective-permute-start(f32[8,384]{1,0:T(8,128)S(1)} %get-tuple-element.108), channel_id=1, source_target_pairs={{32,0},{64,32},{96,64},{128,96},{160,128},{192,160},{224,192},{0,2... | collective-permute-start | bytes 36872 | tf_op jit(solution)/shard_map/ppermute | solution.py:487
  34.3 0.9 shard_map.129
  35.7 2.6 %collective-permute-start.11 = (f32[8,384]{1,0:T(8,128)S(1)}, f32[8,384]{1,0:T(8,128)S(1)}, u32[]{:S(2)}, u32[]{:S(2)}) collective-permute-start(f32[8,384]{1,0:T(8,128)S(1)} %get-tuple-element.166), channel_id=1, source_target_pairs={{1,0},{2,1},{3,2},{4,3},{5,4},{6,5},{7,6},{8,7},{9,8},{10,9},{11,1... | collective-permute-start | bytes 36872 | tf_op jit(solution)/shard_map/ppermute | solution.py:480
  38.3 0.7 shard_map.130.own
  39.7 4.4 %collective-permute-done.10.from_left = f32[8,384]{1,0:T(8,128)S(1)} collective-permute-done((f32[8,384]{1,0:T(8,128)S(1)}, f32[8,384]{1,0:T(8,128)S(1)}, u32[]{:S(2)}, u32[]{:S(2)}) %collective-permute-start.10) | collective-permute-done | bytes 12320 | tf_op jit(solution)/shard_map/ppermute | solution.py:480
  44.6 2.9 %collective-permute-start.13 = (f32[8,384]{1,0:T(8,128)S(1)}, f32[8,384]{1,0:T(8,128)S(1)}, u32[]{:S(2)}, u32[]{:S(2)}) collective-permute-start(f32[8,384]{1,0:T(8,128)S(1)} %get-tuple-element.114), channel_id=1, source_target_pairs={{32,0},{64,32},{96,64},{128,96},{160,128},{192,160},{224,192},{0,2... | collective-permute-start | bytes 36872 | tf_op jit(solution)/shard_map/ppermute | solution.py:487
  47.5 1.2 %shard_map.132 = (f32[192,128]{1,0:T(8,128)S(1)}, f32[8,256]{1,0:T(8,128)S(1)}, f32[8,256]{1,0:T(8,128)S(1)}) custom-call(f32[8,128]{1,0:T(8,128)S(1)} %fusion.3.flags, f32[8,2048]{1,0:T(8,128)S(1)} %get-tuple-element.111.velocity, s32[128,128]{1,0:T(8,128)S(1)} %get-tuple-element.96.places, s32[16,128]{1,0:T(8,128)S(1)} %get-tuple-element.87.list_places), custom_call_target="tpu_custom_call" | custom-call | tf_op jit(solution)/shard_map/pallas_call | solution.py:462
  49.1 1.9 %collective-permute-start.14 = (f32[8,384]{1,0:T(8,128)S(1)}, f32[8,384]{1,0:T(8,128)S(1)}, u32[]{:S(2)}, u32[]{:S(2)}) collective-permute-start(f32[8,384]{1,0:T(8,128)S(1)} %get-tuple-element.165), channel_id=1, source_target_pairs={{0,1},{1,2},{2,3},{3,4},{4,5},{5,6},{6,7},{7,8},{8,9},{9,10},{10,1... | collective-permute-start | bytes 36872 | tf_op jit(solution)/shard_map/ppermute | solution.py:480
  51.0 1.4 %shard_map.133.far_ref = f32[192,128]{1,0:T(8,128)S(1)} custom-call(f32[8,128]{1,0:T(8,128)S(1)} %fusion.3.flags, f32[8,2048]{1,0:T(8,128)S(1)} %get-tuple-element.111.velocity, s32[128,128]{1,0:T(8,128)S(1)} %get-tuple-element.96.places, f32[8,384]{1,0:T(8,128)S(1)} %collective-permute-done.12.from_up, f32[8,384]{1,0:T(8,128)S(1)} %collective-permute-done.13.from_down), custom_call_target="tpu_custom_call" | custom-call | tf_op jit(solution)/shard_map/pallas_call | solution.py:462
  52.7 2.2 %collective-permute-done.14.from_left = f32[8,384]{1,0:T(8,128)S(1)} collective-permute-done((f32[8,384]{1,0:T(8,128)S(1)}, f32[8,384]{1,0:T(8,128)S(1)}, u32[]{:S(2)}, u32[]{:S(2)}) %collective-permute-start.14) | collective-permute-done | bytes 12320 | tf_op jit(solution)/shard_map/ppermute | solution.py:480
  55.6 3.0 %collective-permute-start.17 = (f32[8,384]{1,0:T(8,128)S(1)}, f32[8,384]{1,0:T(8,128)S(1)}, u32[]{:S(2)}, u32[]{:S(2)}) collective-permute-start(f32[8,384]{1,0:T(8,128)S(1)} %get-tuple-element.121), channel_id=1, source_target_pairs={{32,0},{64,32},{96,64},{128,96},{160,128},{192,160},{224,192},{0,2... | collective-permute-start | bytes 36872 | tf_op jit(solution)/shard_map/ppermute | solution.py:487
  58.6 0.9 shard_map.135
  60.0 2.6 %collective-permute-start.19 = (f32[8,384]{1,0:T(8,128)S(1)}, f32[8,384]{1,0:T(8,128)S(1)}, u32[]{:S(2)}, u32[]{:S(2)}) collective-permute-start(f32[8,384]{1,0:T(8,128)S(1)} %get-tuple-element.162), channel_id=1, source_target_pairs={{1,0},{2,1},{3,2},{4,3},{5,4},{6,5},{7,6},{8,7},{9,8},{10,9},{11,1... | collective-permute-start | bytes 36872 | tf_op jit(solution)/shard_map/ppermute | solution.py:480
  62.6 0.7 shard_map.136.own
  64.0 4.4 %collective-permute-done.18.from_left = f32[8,384]{1,0:T(8,128)S(1)} collective-permute-done((f32[8,384]{1,0:T(8,128)S(1)}, f32[8,384]{1,0:T(8,128)S(1)}, u32[]{:S(2)}, u32[]{:S(2)}) %collective-permute-start.18) | collective-permute-done | bytes 12320 | tf_op jit(solution)/shard_map/ppermute | solution.py:480
  68.9 2.9 %collective-permute-start.21 = (f32[8,384]{1,0:T(8,128)S(1)}, f32[8,384]{1,0:T(8,128)S(1)}, u32[]{:S(2)}, u32[]{:S(2)}) collective-permute-start(f32[8,384]{1,0:T(8,128)S(1)} %get-tuple-element.127), channel_id=1, source_target_pairs={{32,0},{64,32},{96,64},{128,96},{160,128},{192,160},{224,192},{0,2... | collective-permute-start | bytes 36872 | tf_op jit(solution)/shard_map/ppermute | solution.py:487
  71.8 1.2 %shard_map.138 = (f32[192,128]{1,0:T(8,128)S(1)}, f32[8,256]{1,0:T(8,128)S(1)}, f32[8,256]{1,0:T(8,128)S(1)}) custom-call(f32[8,128]{1,0:T(8,128)S(1)} %fusion.3.flags, f32[8,2048]{1,0:T(8,128)S(1)} %get-tuple-element.124.velocity, s32[128,128]{1,0:T(8,128)S(1)} %get-tuple-element.96.places, s32[16,128]{1,0:T(8,128)S(1)} %get-tuple-element.87.list_places), custom_call_target="tpu_custom_call" | custom-call | tf_op jit(solution)/shard_map/pallas_call | solution.py:462
  73.4 1.9 %collective-permute-start.22 = (f32[8,384]{1,0:T(8,128)S(1)}, f32[8,384]{1,0:T(8,128)S(1)}, u32[]{:S(2)}, u32[]{:S(2)}) collective-permute-start(f32[8,384]{1,0:T(8,128)S(1)} %get-tuple-element.161), channel_id=1, source_target_pairs={{0,1},{1,2},{2,3},{3,4},{4,5},{5,6},{6,7},{7,8},{8,9},{9,10},{10,1... | collective-permute-start | bytes 36872 | tf_op jit(solution)/shard_map/ppermute | solution.py:480
  75.3 1.4 %shard_map.139.far_ref = f32[192,128]{1,0:T(8,128)S(1)} custom-call(f32[8,128]{1,0:T(8,128)S(1)} %fusion.3.flags, f32[8,2048]{1,0:T(8,128)S(1)} %get-tuple-element.124.velocity, s32[128,128]{1,0:T(8,128)S(1)} %get-tuple-element.96.places, f32[8,384]{1,0:T(8,128)S(1)} %collective-permute-done.20.from_up, f32[8,384]{1,0:T(8,128)S(1)} %collective-permute-done.21.from_down), custom_call_target="tpu_custom_call" | custom-call | tf_op jit(solution)/shard_map/pallas_call | solution.py:462
  77.0 2.2 %collective-permute-done.22.from_left = f32[8,384]{1,0:T(8,128)S(1)} collective-permute-done((f32[8,384]{1,0:T(8,128)S(1)}, f32[8,384]{1,0:T(8,128)S(1)}, u32[]{:S(2)}, u32[]{:S(2)}) %collective-permute-start.22) | collective-permute-done | bytes 12320 | tf_op jit(solution)/shard_map/ppermute | solution.py:480
  80.0 3.0 %collective-permute-start.25 = (f32[8,384]{1,0:T(8,128)S(1)}, f32[8,384]{1,0:T(8,128)S(1)}, u32[]{:S(2)}, u32[]{:S(2)}) collective-permute-start(f32[8,384]{1,0:T(8,128)S(1)} %get-tuple-element.134), channel_id=1, source_target_pairs={{32,0},{64,32},{96,64},{128,96},{160,128},{192,160},{224,192},{0,2... | collective-permute-start | bytes 36872 | tf_op jit(solution)/shard_map/ppermute | solution.py:487
  82.9 0.9 shard_map.141
  84.3 2.8 %collective-permute-start.27 = (f32[8,384]{1,0:T(8,128)S(1)}, f32[8,384]{1,0:T(8,128)S(1)}, u32[]{:S(2)}, u32[]{:S(2)}) collective-permute-start(f32[8,384]{1,0:T(8,128)S(1)} %get-tuple-element.158), channel_id=1, source_target_pairs={{1,0},{2,1},{3,2},{4,3},{5,4},{6,5},{7,6},{8,7},{9,8},{10,9},{11,1... | collective-permute-start | bytes 36872 | tf_op jit(solution)/shard_map/ppermute | solution.py:480
  87.1 0.7 shard_map.142.own
  88.5 4.4 %collective-permute-done.26.from_left = f32[8,384]{1,0:T(8,128)S(1)} collective-permute-done((f32[8,384]{1,0:T(8,128)S(1)}, f32[8,384]{1,0:T(8,128)S(1)}, u32[]{:S(2)}, u32[]{:S(2)}) %collective-permute-start.26) | collective-permute-done | bytes 12320 | tf_op jit(solution)/shard_map/ppermute | solution.py:480
  93.4 2.9 %collective-permute-start.29 = (f32[8,384]{1,0:T(8,128)S(1)}, f32[8,384]{1,0:T(8,128)S(1)}, u32[]{:S(2)}, u32[]{:S(2)}) collective-permute-start(f32[8,384]{1,0:T(8,128)S(1)} %get-tuple-element.140), channel_id=1, source_target_pairs={{32,0},{64,32},{96,64},{128,96},{160,128},{192,160},{224,192},{0,2... | collective-permute-start | bytes 36872 | tf_op jit(solution)/shard_map/ppermute | solution.py:487
  96.3 1.2 %shard_map.144 = (f32[192,128]{1,0:T(8,128)S(1)}, f32[8,256]{1,0:T(8,128)S(1)}, f32[8,256]{1,0:T(8,128)S(1)}) custom-call(f32[8,128]{1,0:T(8,128)S(1)} %fusion.3.flags, f32[8,2048]{1,0:T(8,128)S(1)} %get-tuple-element.137.velocity, s32[128,128]{1,0:T(8,128)S(1)} %get-tuple-element.96.places, s32[16,128]{1,0:T(8,128)S(1)} %get-tuple-element.87.list_places), custom_call_target="tpu_custom_call" | custom-call | tf_op jit(solution)/shard_map/pallas_call | solution.py:462
  97.8 2.0 %collective-permute-start.30 = (f32[8,384]{1,0:T(8,128)S(1)}, f32[8,384]{1,0:T(8,128)S(1)}, u32[]{:S(2)}, u32[]{:S(2)}) collective-permute-start(f32[8,384]{1,0:T(8,128)S(1)} %get-tuple-element.157), channel_id=1, source_target_pairs={{0,1},{1,2},{2,3},{3,4},{4,5},{5,6},{6,7},{7,8},{8,9},{9,10},{10,1... | collective-permute-start | bytes 36872 | tf_op jit(solution)/shard_map/ppermute | solution.py:480
  99.8 1.4 %shard_map.145.far_ref = f32[192,128]{1,0:T(8,128)S(1)} custom-call(f32[8,128]{1,0:T(8,128)S(1)} %fusion.3.flags, f32[8,2048]{1,0:T(8,128)S(1)} %get-tuple-element.137.velocity, s32[128,128]{1,0:T(8,128)S(1)} %get-tuple-element.96.places, f32[8,384]{1,0:T(8,128)S(1)} %collective-permute-done.28.from_up, f32[8,384]{1,0:T(8,128)S(1)} %collective-permute-done.29.from_down), custom_call_target="tpu_custom_call" | custom-call | tf_op jit(solution)/shard_map/pallas_call | solution.py:462
  101.5 2.2 %collective-permute-done.30.from_left = f32[8,384]{1,0:T(8,128)S(1)} collective-permute-done((f32[8,384]{1,0:T(8,128)S(1)}, f32[8,384]{1,0:T(8,128)S(1)}, u32[]{:S(2)}, u32[]{:S(2)}) %collective-permute-start.30) | collective-permute-done | bytes 12320 | tf_op jit(solution)/shard_map/ppermute | solution.py:480
  103.7 1.2 %shard_map.146 = (f32[96,128]{1,0:T(8,128)}, f32[256,128]{1,0:T(8,128)S(1)}, f32[8,384]{1,0:T(8,128)S(1)}, f32[8,384]{1,0:T(8,128)S(1)}) custom-call(f32[8,128]{1,0:T(8,128)S(1)} %fusion.3.flags, f32[192,128]{1,0:T(8,128)S(1)} %get-tuple-element.138.near_ref, f32[192,128]{1,0:T(8,128)S(1)} %shard_map.145.far_ref, f32[416,128]{1,0:T(8,128)S(1)} %get-tuple-element.80.table, ...), custom_call_target="tpu_custom_call" | custom-call | tf_op jit(solution)/shard_map/pallas_call | solution.py:462
  104.9 3.0 %collective-permute-start.33 = (f32[8,384]{1,0:T(8,128)S(1)}, f32[8,384]{1,0:T(8,128)S(1)}, u32[]{:S(2)}, u32[]{:S(2)}) collective-permute-start(f32[8,384]{1,0:T(8,128)S(1)} %get-tuple-element.147), channel_id=1, source_target_pairs={{32,0},{64,32},{96,64},{128,96},{160,128},{192,160},{224,192},{0,2... | collective-permute-start | bytes 36872 | tf_op jit(solution)/shard_map/ppermute | solution.py:487
  107.9 0.8 copy-done
  108.7 0.9 shard_map.147
  109.6 2.6 %collective-permute-start.35 = (f32[8,384]{1,0:T(8,128)S(1)}, f32[8,384]{1,0:T(8,128)S(1)}, u32[]{:S(2)}, u32[]{:S(2)}) collective-permute-start(f32[8,384]{1,0:T(8,128)S(1)} %get-tuple-element.154), channel_id=1, source_target_pairs={{1,0},{2,1},{3,2},{4,3},{5,4},{6,5},{7,6},{8,7},{9,8},{10,9},{11,1... | collective-permute-start | bytes 36872 | tf_op jit(solution)/shard_map/ppermute | solution.py:480
  112.3 0.7 shard_map.148.own
  113.7 4.4 %collective-permute-done.34.from_left = f32[8,384]{1,0:T(8,128)S(1)} collective-permute-done((f32[8,384]{1,0:T(8,128)S(1)}, f32[8,384]{1,0:T(8,128)S(1)}, u32[]{:S(2)}, u32[]{:S(2)}) %collective-permute-start.34) | collective-permute-done | bytes 12320 | tf_op jit(solution)/shard_map/ppermute | solution.py:480
  118.1 0.9 shard_map.149
  (79 shorter events, 12.1 us)
Async XLA Ops:
  3.1 4.6 %collective-permute-start = (f32[8,384]{1,0:T(8,128)S(1)}, f32[8,384]{1,0:T(8,128)S(1)}, u32[]{:S(2)}, u32[]{:S(2)}) collective-permute-start(f32[8,384]{1,0:T(8,128)S(1)} %get-tuple-element.89), channel_id=1, source_target_pairs={{0,32},{32,64},{64,96},{96,128},{128,160},{160,192},{192,224},{224... | collective-permute-start | bytes 36872 | tf_op jit(solution)/shard_map/ppermute | solution.py:487
  3.1 4.6 %collective-permute-start.1 = (f32[8,384]{1,0:T(8,128)S(1)}, f32[8,384]{1,0:T(8,128)S(1)}, u32[]{:S(2)}, u32[]{:S(2)}) collective-permute-start(f32[8,384]{1,0:T(8,128)S(1)} %get-tuple-element.90), channel_id=1, source_target_pairs={{32,0},{64,32},{96,64},{128,96},{160,128},{192,160},{224,192},{0,2... | collective-permute-start | bytes 36872 | tf_op jit(solution)/shard_map/ppermute | solution.py:487
  7.8 7.6 %collective-permute-start.3 = (f32[8,384]{1,0:T(8,128)S(1)}, f32[8,384]{1,0:T(8,128)S(1)}, u32[]{:S(2)}, u32[]{:S(2)}) collective-permute-start(f32[8,384]{1,0:T(8,128)S(1)} %get-tuple-element.170), channel_id=1, source_target_pairs={{1,0},{2,1},{3,2},{4,3},{5,4},{6,5},{7,6},{8,7},{9,8},{10,9},{11,1... | collective-permute-start | bytes 36872 | tf_op jit(solution)/shard_map/ppermute | solution.py:480
  14.0 5.8 %collective-permute-start.2 = (f32[8,384]{1,0:T(8,128)S(1)}, f32[8,384]{1,0:T(8,128)S(1)}, u32[]{:S(2)}, u32[]{:S(2)}) collective-permute-start(f32[8,384]{1,0:T(8,128)S(1)} %get-tuple-element.171), channel_id=1, source_target_pairs={{0,1},{1,2},{2,3},{3,4},{4,5},{5,6},{6,7},{7,8},{8,9},{9,10},{10,1... | collective-permute-start | bytes 36872 | tf_op jit(solution)/shard_map/ppermute | solution.py:480
  20.2 4.3 %collective-permute-start.4 = (f32[8,384]{1,0:T(8,128)S(1)}, f32[8,384]{1,0:T(8,128)S(1)}, u32[]{:S(2)}, u32[]{:S(2)}) collective-permute-start(f32[8,384]{1,0:T(8,128)S(1)} %get-tuple-element.98), channel_id=1, source_target_pairs={{0,32},{32,64},{64,96},{96,128},{128,160},{160,192},{192,224},{224... | collective-permute-start | bytes 36872 | tf_op jit(solution)/shard_map/ppermute | solution.py:487
  20.3 4.3 %collective-permute-start.5 = (f32[8,384]{1,0:T(8,128)S(1)}, f32[8,384]{1,0:T(8,128)S(1)}, u32[]{:S(2)}, u32[]{:S(2)}) collective-permute-start(f32[8,384]{1,0:T(8,128)S(1)} %get-tuple-element.99), channel_id=1, source_target_pairs={{32,0},{64,32},{96,64},{128,96},{160,128},{192,160},{224,192},{0,2... | collective-permute-start | bytes 36872 | tf_op jit(solution)/shard_map/ppermute | solution.py:487
  24.6 3.7 %collective-permute-start.7 = (f32[8,384]{1,0:T(8,128)S(1)}, f32[8,384]{1,0:T(8,128)S(1)}, u32[]{:S(2)}, u32[]{:S(2)}) collective-permute-start(f32[8,384]{1,0:T(8,128)S(1)} %get-tuple-element.168), channel_id=1, source_target_pairs={{1,0},{2,1},{3,2},{4,3},{5,4},{6,5},{7,6},{8,7},{9,8},{10,9},{11,1... | collective-permute-start | bytes 36872 | tf_op jit(solution)/shard_map/ppermute | solution.py:480
  24.7 5.9 %collective-permute-start.6 = (f32[8,384]{1,0:T(8,128)S(1)}, f32[8,384]{1,0:T(8,128)S(1)}, u32[]{:S(2)}, u32[]{:S(2)}) collective-permute-start(f32[8,384]{1,0:T(8,128)S(1)} %get-tuple-element.169), channel_id=1, source_target_pairs={{0,1},{1,2},{2,3},{3,4},{4,5},{5,6},{6,7},{7,8},{8,9},{9,10},{10,1... | collective-permute-start | bytes 36872 | tf_op jit(solution)/shard_map/ppermute | solution.py:480
  31.3 4.4 %collective-permute-start.8 = (f32[8,384]{1,0:T(8,128)S(1)}, f32[8,384]{1,0:T(8,128)S(1)}, u32[]{:S(2)}, u32[]{:S(2)}) collective-permute-start(f32[8,384]{1,0:T(8,128)S(1)} %get-tuple-element.107), channel_id=1, source_target_pairs={{0,32},{32,64},{64,96},{96,128},{128,160},{160,192},{192,224},{224... | collective-permute-start | bytes 36872 | tf_op jit(solution)/shard_map/ppermute | solution.py:487
  31.3 4.4 %collective-permute-start.9 = (f32[8,384]{1,0:T(8,128)S(1)}, f32[8,384]{1,0:T(8,128)S(1)}, u32[]{:S(2)}, u32[]{:S(2)}) collective-permute-start(f32[8,384]{1,0:T(8,128)S(1)} %get-tuple-element.108), channel_id=1, source_target_pairs={{32,0},{64,32},{96,64},{128,96},{160,128},{192,160},{224,192},{0,2... | collective-permute-start | bytes 36872 | tf_op jit(solution)/shard_map/ppermute | solution.py:487
  35.7 4.0 %collective-permute-start.11 = (f32[8,384]{1,0:T(8,128)S(1)}, f32[8,384]{1,0:T(8,128)S(1)}, u32[]{:S(2)}, u32[]{:S(2)}) collective-permute-start(f32[8,384]{1,0:T(8,128)S(1)} %get-tuple-element.166), channel_id=1, source_target_pairs={{1,0},{2,1},{3,2},{4,3},{5,4},{6,5},{7,6},{8,7},{9,8},{10,9},{11,1... | collective-permute-start | bytes 36872 | tf_op jit(solution)/shard_map/ppermute | solution.py:480
  38.3 5.8 %collective-permute-start.10 = (f32[8,384]{1,0:T(8,128)S(1)}, f32[8,384]{1,0:T(8,128)S(1)}, u32[]{:S(2)}, u32[]{:S(2)}) collective-permute-start(f32[8,384]{1,0:T(8,128)S(1)} %get-tuple-element.167), channel_id=1, source_target_pairs={{0,1},{1,2},{2,3},{3,4},{4,5},{5,6},{6,7},{7,8},{8,9},{9,10},{10,1... | collective-permute-start | bytes 36872 | tf_op jit(solution)/shard_map/ppermute | solution.py:480
  44.6 4.3 %collective-permute-start.12 = (f32[8,384]{1,0:T(8,128)S(1)}, f32[8,384]{1,0:T(8,128)S(1)}, u32[]{:S(2)}, u32[]{:S(2)}) collective-permute-start(f32[8,384]{1,0:T(8,128)S(1)} %get-tuple-element.113), channel_id=1, source_target_pairs={{0,32},{32,64},{64,96},{96,128},{128,160},{160,192},{192,224},{224... | collective-permute-start | bytes 36872 | tf_op jit(solution)/shard_map/ppermute | solution.py:487
  44.6 4.3 %collective-permute-start.13 = (f32[8,384]{1,0:T(8,128)S(1)}, f32[8,384]{1,0:T(8,128)S(1)}, u32[]{:S(2)}, u32[]{:S(2)}) collective-permute-start(f32[8,384]{1,0:T(8,128)S(1)} %get-tuple-element.114), channel_id=1, source_target_pairs={{32,0},{64,32},{96,64},{128,96},{160,128},{192,160},{224,192},{0,2... | collective-permute-start | bytes 36872 | tf_op jit(solution)/shard_map/ppermute | solution.py:487
  48.9 3.7 %collective-permute-start.15 = (f32[8,384]{1,0:T(8,128)S(1)}, f32[8,384]{1,0:T(8,128)S(1)}, u32[]{:S(2)}, u32[]{:S(2)}) collective-permute-start(f32[8,384]{1,0:T(8,128)S(1)} %get-tuple-element.164), channel_id=1, source_target_pairs={{1,0},{2,1},{3,2},{4,3},{5,4},{6,5},{7,6},{8,7},{9,8},{10,9},{11,1... | collective-permute-start | bytes 36872 | tf_op jit(solution)/shard_map/ppermute | solution.py:480
  49.1 5.8 %collective-permute-start.14 = (f32[8,384]{1,0:T(8,128)S(1)}, f32[8,384]{1,0:T(8,128)S(1)}, u32[]{:S(2)}, u32[]{:S(2)}) collective-permute-start(f32[8,384]{1,0:T(8,128)S(1)} %get-tuple-element.165), channel_id=1, source_target_pairs={{0,1},{1,2},{2,3},{3,4},{4,5},{5,6},{6,7},{7,8},{8,9},{9,10},{10,1... | collective-permute-start | bytes 36872 | tf_op jit(solution)/shard_map/ppermute | solution.py:480
  55.6 4.4 %collective-permute-start.16 = (f32[8,384]{1,0:T(8,128)S(1)}, f32[8,384]{1,0:T(8,128)S(1)}, u32[]{:S(2)}, u32[]{:S(2)}) collective-permute-start(f32[8,384]{1,0:T(8,128)S(1)} %get-tuple-element.120), channel_id=1, source_target_pairs={{0,32},{32,64},{64,96},{96,128},{128,160},{160,192},{192,224},{224... | collective-permute-start | bytes 36872 | tf_op jit(solution)/shard_map/ppermute | solution.py:487
  55.6 4.4 %collective-permute-start.17 = (f32[8,384]{1,0:T(8,128)S(1)}, f32[8,384]{1,0:T(8,128)S(1)}, u32[]{:S(2)}, u32[]{:S(2)}) collective-permute-start(f32[8,384]{1,0:T(8,128)S(1)} %get-tuple-element.121), channel_id=1, source_target_pairs={{32,0},{64,32},{96,64},{128,96},{160,128},{192,160},{224,192},{0,2... | collective-permute-start | bytes 36872 | tf_op jit(solution)/shard_map/ppermute | solution.py:487
  60.0 4.0 %collective-permute-start.19 = (f32[8,384]{1,0:T(8,128)S(1)}, f32[8,384]{1,0:T(8,128)S(1)}, u32[]{:S(2)}, u32[]{:S(2)}) collective-permute-start(f32[8,384]{1,0:T(8,128)S(1)} %get-tuple-element.162), channel_id=1, source_target_pairs={{1,0},{2,1},{3,2},{4,3},{5,4},{6,5},{7,6},{8,7},{9,8},{10,9},{11,1... | collective-permute-start | bytes 36872 | tf_op jit(solution)/shard_map/ppermute | solution.py:480
  62.6 5.8 %collective-permute-start.18 = (f32[8,384]{1,0:T(8,128)S(1)}, f32[8,384]{1,0:T(8,128)S(1)}, u32[]{:S(2)}, u32[]{:S(2)}) collective-permute-start(f32[8,384]{1,0:T(8,128)S(1)} %get-tuple-element.163), channel_id=1, source_target_pairs={{0,1},{1,2},{2,3},{3,4},{4,5},{5,6},{6,7},{7,8},{8,9},{9,10},{10,1... | collective-permute-start | bytes 36872 | tf_op jit(solution)/shard_map/ppermute | solution.py:480
  68.9 4.3 %collective-permute-start.20 = (f32[8,384]{1,0:T(8,128)S(1)}, f32[8,384]{1,0:T(8,128)S(1)}, u32[]{:S(2)}, u32[]{:S(2)}) collective-permute-start(f32[8,384]{1,0:T(8,128)S(1)} %get-tuple-element.126), channel_id=1, source_target_pairs={{0,32},{32,64},{64,96},{96,128},{128,160},{160,192},{192,224},{224... | collective-permute-start | bytes 36872 | tf_op jit(solution)/shard_map/ppermute | solution.py:487
  68.9 4.3 %collective-permute-start.21 = (f32[8,384]{1,0:T(8,128)S(1)}, f32[8,384]{1,0:T(8,128)S(1)}, u32[]{:S(2)}, u32[]{:S(2)}) collective-permute-start(f32[8,384]{1,0:T(8,128)S(1)} %get-tuple-element.127), channel_id=1, source_target_pairs={{32,0},{64,32},{96,64},{128,96},{160,128},{192,160},{224,192},{0,2... | collective-permute-start | bytes 36872 | tf_op jit(solution)/shard_map/ppermute | solution.py:487
  73.2 3.7 %collective-permute-start.23 = (f32[8,384]{1,0:T(8,128)S(1)}, f32[8,384]{1,0:T(8,128)S(1)}, u32[]{:S(2)}, u32[]{:S(2)}) collective-permute-start(f32[8,384]{1,0:T(8,128)S(1)} %get-tuple-element.160), channel_id=1, source_target_pairs={{1,0},{2,1},{3,2},{4,3},{5,4},{6,5},{7,6},{8,7},{9,8},{10,9},{11,1... | collective-permute-start | bytes 36872 | tf_op jit(solution)/shard_map/ppermute | solution.py:480
  73.4 5.8 %collective-permute-start.22 = (f32[8,384]{1,0:T(8,128)S(1)}, f32[8,384]{1,0:T(8,128)S(1)}, u32[]{:S(2)}, u32[]{:S(2)}) collective-permute-start(f32[8,384]{1,0:T(8,128)S(1)} %get-tuple-element.161), channel_id=1, source_target_pairs={{0,1},{1,2},{2,3},{3,4},{4,5},{5,6},{6,7},{7,8},{8,9},{9,10},{10,1... | collective-permute-start | bytes 36872 | tf_op jit(solution)/shard_map/ppermute | solution.py:480
  79.9 4.4 %collective-permute-start.24 = (f32[8,384]{1,0:T(8,128)S(1)}, f32[8,384]{1,0:T(8,128)S(1)}, u32[]{:S(2)}, u32[]{:S(2)}) collective-permute-start(f32[8,384]{1,0:T(8,128)S(1)} %get-tuple-element.133), channel_id=1, source_target_pairs={{0,32},{32,64},{64,96},{96,128},{128,160},{160,192},{192,224},{224... | collective-permute-start | bytes 36872 | tf_op jit(solution)/shard_map/ppermute | solution.py:487
  80.0 4.4 %collective-permute-start.25 = (f32[8,384]{1,0:T(8,128)S(1)}, f32[8,384]{1,0:T(8,128)S(1)}, u32[]{:S(2)}, u32[]{:S(2)}) collective-permute-start(f32[8,384]{1,0:T(8,128)S(1)} %get-tuple-element.134), channel_id=1, source_target_pairs={{32,0},{64,32},{96,64},{128,96},{160,128},{192,160},{224,192},{0,2... | collective-permute-start | bytes 36872 | tf_op jit(solution)/shard_map/ppermute | solution.py:487
  84.3 4.2 %collective-permute-start.27 = (f32[8,384]{1,0:T(8,128)S(1)}, f32[8,384]{1,0:T(8,128)S(1)}, u32[]{:S(2)}, u32[]{:S(2)}) collective-permute-start(f32[8,384]{1,0:T(8,128)S(1)} %get-tuple-element.158), channel_id=1, source_target_pairs={{1,0},{2,1},{3,2},{4,3},{5,4},{6,5},{7,6},{8,7},{9,8},{10,9},{11,1... | collective-permute-start | bytes 36872 | tf_op jit(solution)/shard_map/ppermute | solution.py:480
  87.1 5.8 %collective-permute-start.26 = (f32[8,384]{1,0:T(8,128)S(1)}, f32[8,384]{1,0:T(8,128)S(1)}, u32[]{:S(2)}, u32[]{:S(2)}) collective-permute-start(f32[8,384]{1,0:T(8,128)S(1)} %get-tuple-element.159), channel_id=1, source_target_pairs={{0,1},{1,2},{2,3},{3,4},{4,5},{5,6},{6,7},{7,8},{8,9},{9,10},{10,1... | collective-permute-start | bytes 36872 | tf_op jit(solution)/shard_map/ppermute | solution.py:480
  93.4 4.3 %collective-permute-start.28 = (f32[8,384]{1,0:T(8,128)S(1)}, f32[8,384]{1,0:T(8,128)S(1)}, u32[]{:S(2)}, u32[]{:S(2)}) collective-permute-start(f32[8,384]{1,0:T(8,128)S(1)} %get-tuple-element.139), channel_id=1, source_target_pairs={{0,32},{32,64},{64,96},{96,128},{128,160},{160,192},{192,224},{224... | collective-permute-start | bytes 36872 | tf_op jit(solution)/shard_map/ppermute | solution.py:487
  93.4 4.3 %collective-permute-start.29 = (f32[8,384]{1,0:T(8,128)S(1)}, f32[8,384]{1,0:T(8,128)S(1)}, u32[]{:S(2)}, u32[]{:S(2)}) collective-permute-start(f32[8,384]{1,0:T(8,128)S(1)} %get-tuple-element.140), channel_id=1, source_target_pairs={{32,0},{64,32},{96,64},{128,96},{160,128},{192,160},{224,192},{0,2... | collective-permute-start | bytes 36872 | tf_op jit(solution)/shard_map/ppermute | solution.py:487
  97.8 3.7 %collective-permute-start.31 = (f32[8,384]{1,0:T(8,128)S(1)}, f32[8,384]{1,0:T(8,128)S(1)}, u32[]{:S(2)}, u32[]{:S(2)}) collective-permute-start(f32[8,384]{1,0:T(8,128)S(1)} %get-tuple-element.156), channel_id=1, source_target_pairs={{1,0},{2,1},{3,2},{4,3},{5,4},{6,5},{7,6},{8,7},{9,8},{10,9},{11,1... | collective-permute-start | bytes 36872 | tf_op jit(solution)/shard_map/ppermute | solution.py:480
  97.8 5.9 %collective-permute-start.30 = (f32[8,384]{1,0:T(8,128)S(1)}, f32[8,384]{1,0:T(8,128)S(1)}, u32[]{:S(2)}, u32[]{:S(2)}) collective-permute-start(f32[8,384]{1,0:T(8,128)S(1)} %get-tuple-element.157), channel_id=1, source_target_pairs={{0,1},{1,2},{2,3},{3,4},{4,5},{5,6},{6,7},{7,8},{8,9},{9,10},{10,1... | collective-permute-start | bytes 36872 | tf_op jit(solution)/shard_map/ppermute | solution.py:480
  104.9 4.7 %collective-permute-start.32 = (f32[8,384]{1,0:T(8,128)S(1)}, f32[8,384]{1,0:T(8,128)S(1)}, u32[]{:S(2)}, u32[]{:S(2)}) collective-permute-start(f32[8,384]{1,0:T(8,128)S(1)} %get-tuple-element.146), channel_id=1, source_target_pairs={{0,32},{32,64},{64,96},{96,128},{128,160},{160,192},{192,224},{224... | collective-permute-start | bytes 36872 | tf_op jit(solution)/shard_map/ppermute | solution.py:487
  104.9 4.7 %collective-permute-start.33 = (f32[8,384]{1,0:T(8,128)S(1)}, f32[8,384]{1,0:T(8,128)S(1)}, u32[]{:S(2)}, u32[]{:S(2)}) collective-permute-start(f32[8,384]{1,0:T(8,128)S(1)} %get-tuple-element.147), channel_id=1, source_target_pairs={{32,0},{64,32},{96,64},{128,96},{160,128},{192,160},{224,192},{0,2... | collective-permute-start | bytes 36872 | tf_op jit(solution)/shard_map/ppermute | solution.py:487
  107.9 0.8 copy-start
  109.6 4.0 %collective-permute-start.35 = (f32[8,384]{1,0:T(8,128)S(1)}, f32[8,384]{1,0:T(8,128)S(1)}, u32[]{:S(2)}, u32[]{:S(2)}) collective-permute-start(f32[8,384]{1,0:T(8,128)S(1)} %get-tuple-element.154), channel_id=1, source_target_pairs={{1,0},{2,1},{3,2},{4,3},{5,4},{6,5},{7,6},{8,7},{9,8},{10,9},{11,1... | collective-permute-start | bytes 36872 | tf_op jit(solution)/shard_map/ppermute | solution.py:480
  112.2 5.8 %collective-permute-start.34 = (f32[8,384]{1,0:T(8,128)S(1)}, f32[8,384]{1,0:T(8,128)S(1)}, u32[]{:S(2)}, u32[]{:S(2)}) collective-permute-start(f32[8,384]{1,0:T(8,128)S(1)} %get-tuple-element.155), channel_id=1, source_target_pairs={{0,1},{1,2},{2,3},{3,4},{4,5},{5,6},{6,7},{7,8},{8,9},{9,10},{10,1... | collective-permute-start | bytes 36872 | tf_op jit(solution)/shard_map/ppermute | solution.py:480
